TPU v7x, 512 devices: a whole 4x8x8 slice. The times are simulated.
512 devices in a mesh: resp: 8 (over y), fsdp: 64 (over x, z, core).
Axes of the slice: x: 4, y: 8, z: 8, core: 2. Of those that a mesh axis runs over, the one named last changes fastest.
Arguments:
- queries: bfloat16 [64, 1024, 2560], P('fsdp', 'resp'), may hold values from -130 to 130
- resp_keys: bfloat16 [64, 1024, 512], P('fsdp', 'resp'), may hold values from -6 to 6
- response_values: bfloat16 [64, 1024, 512], P('fsdp', 'resp'), may hold values from -6 to 6
- rotated_prompt_keys: bfloat16 [64, 128, 512], P('fsdp', 'resp'), may hold values from -6 to 6
- prompt_value_rows: bfloat16 [64, 128, 512], P('fsdp', 'resp'), may hold values from -6 to 6
- attention_output_gradient: bfloat16 [64, 1024, 2560], P('fsdp', 'resp'), may hold values from -6 to 6
- output_grad: bfloat16 [64, 1024, 5120], P('fsdp', 'resp'), may hold values from -6 to 6
- advantages: float32 [64, 8], P('fsdp', 'resp'), may hold values from -4 to 4
- lengths: int32 [64, 8], P('fsdp'), may hold values from 1 to 128, as said below
- tree_mask: int32 [64, 16, 16], P('fsdp'), may hold values from 0 to 1, as said below
- adapter: float32 [16, 7680], P(None, 'fsdp'), may hold values from -0.3 to 0.3
- first_moment: float32 [16, 7680], P(None, 'fsdp'), may hold values from -0.013671875 to 0.013671875
- second_moment: float32 [16, 7680], P(None, 'fsdp'), may hold values from 1.6276042e-09 to 1.6276041e-07
Outputs:
- query_grad: bfloat16 [64, 1024, 2560], P('fsdp', 'resp')
- key_grad: bfloat16 [64, 1024, 512], P('fsdp', 'resp')
- value_grad: bfloat16 [64, 1024, 512], P('fsdp', 'resp')
- prompt_key_grad: bfloat16 [64, 128, 512], P('fsdp', 'resp')
- prompt_value_grad: bfloat16 [64, 128, 512], P('fsdp', 'resp')
- adam_update: float32 [16, 7680], P(None, 'fsdp')
Inputs may be any that keep to these rules, and one draw needn't show every extreme that they name: `lengths`: in every group some response has exactly 128 tokens. Each group's blocks form a forest: every block but a response's first hangs on the block before it, a response's first block hangs on no block or on a block of a lower-numbered response of its group; tree_mask[g, b, c] is 1 where c is b or one of its ancestors, else 0.
All inputs are finite; a program needn't handle non-finite values.
Results may differ from a plain program's by a relative error of at most 0.018.
Values may be sent and summed in bfloat16 or wider, within the bound.
No kernel may reach another device: no remote copies, remote signals or barrier semaphores. Data moves between devices by JAX's collectives and lax.ppermute only.
A program may use at most 128 MiB of HBM per device.

v0:
```python
import jax
import jax.numpy as jnp
from jax import lax
from jax.sharding import PartitionSpec as P

HEAD_SIZE = 128
QUERY_HEADS = 20
KEY_VALUE_HEADS = 4
BLK = 64
RESPONSE_TOKENS = 128


adapter_scale = 2.0
max_norm = 1.0
beta_first = 0.9
beta_second = 0.999
first_fix = 0.9999734386011124
second_fix = 0.0952078516
adam_eps = 1e-08


def visible(resp_index, lengths_row, tree_rows, n_resp, prefix_rows):
    per_resp = RESPONSE_TOKENS // BLK
    query_pos = jnp.arange(RESPONSE_TOKENS, dtype=jnp.int32)
    query_blk = resp_index * per_resp + query_pos // BLK
    key_col = jnp.arange(n_resp * RESPONSE_TOKENS, dtype=jnp.int32)
    key_pos = key_col % RESPONSE_TOKENS
    key_blk = key_col // BLK
    tree_bits = jnp.repeat(jnp.repeat(tree_rows, BLK, axis=1), BLK, axis=0)
    key_limit = jnp.repeat(lengths_row, RESPONSE_TOKENS)
    inside = (tree_bits == 1) & (key_pos[None, :] < key_limit[None, :])
    causal = (key_blk[None, :] != query_blk[:, None]) | (key_pos[None, :] <= query_pos[:, None])
    return jnp.concatenate(
        [jnp.ones((RESPONSE_TOKENS, prefix_rows), jnp.bool_), inside & causal], axis=1
    )


def attend_heads(queries, all_keys, all_values, allowed, attention_cotangent):
    group_members = QUERY_HEADS // KEY_VALUE_HEADS
    score_scale = HEAD_SIZE ** (-0.5)
    outputs = []
    query_parts = []
    key_parts = []
    value_parts = []
    for current_head_index in range(KEY_VALUE_HEADS):
        columns = slice(
            current_head_index * group_members * HEAD_SIZE,
            (current_head_index + 1) * group_members * HEAD_SIZE,
        )
        query_head = queries[:, columns].reshape(RESPONSE_TOKENS, group_members, HEAD_SIZE)
        grad_head = attention_cotangent[:, columns].reshape(
            RESPONSE_TOKENS, group_members, HEAD_SIZE
        )
        key_head = all_keys[
            :, current_head_index * HEAD_SIZE : (current_head_index + 1) * HEAD_SIZE
        ]
        value_head = all_values[
            :, current_head_index * HEAD_SIZE : (current_head_index + 1) * HEAD_SIZE
        ]
        scores = (
            jnp.einsum("tgd,kd->gtk", query_head, key_head, preferred_element_type=jnp.float32)
            * score_scale
        )
        scores = jnp.where(allowed[None], scores, -jnp.inf)
        peak_value = jnp.max(scores, axis=2, keepdims=True)
        row_total = jnp.sum(jnp.exp(scores - peak_value), axis=2, keepdims=True)
        log_sum = peak_value + jnp.log(row_total)
        weights = jnp.exp(scores - log_sum)
        weight_half = weights.astype(jnp.bfloat16)
        head_out = jnp.einsum(
            "gtk,kd->tgd", weight_half, value_head, preferred_element_type=jnp.float32
        ).astype(jnp.bfloat16)
        outputs.append(head_out.reshape(RESPONSE_TOKENS, group_members * HEAD_SIZE))
        value_parts.append(
            jnp.einsum("gtk,tgd->kd", weight_half, grad_head, preferred_element_type=jnp.float32)
        )
        weight_grad = jnp.einsum(
            "tgd,kd->gtk", grad_head, value_head, preferred_element_type=jnp.float32
        )
        inner = jnp.transpose(
            jnp.sum(grad_head.astype(jnp.float32) * head_out.astype(jnp.float32), axis=2)
        )[:, :, None]
        score_grad = (weights * (weight_grad - inner) * score_scale).astype(jnp.bfloat16)
        query_parts.append(
            jnp.einsum(
                "gtk,kd->tgd", score_grad, key_head, preferred_element_type=jnp.float32
            ).reshape(RESPONSE_TOKENS, group_members * HEAD_SIZE)
        )
        key_parts.append(
            jnp.einsum("gtk,tgd->kd", score_grad, query_head, preferred_element_type=jnp.float32)
        )
    return (
        jnp.concatenate(outputs, axis=1),
        jnp.concatenate(query_parts, axis=1),
        jnp.concatenate(key_parts, axis=1),
        jnp.concatenate(value_parts, axis=1),
    )


def local_pass(
    queries,
    attention_output_gradient,
    output_grad,
    advantage,
    own_length,
    lengths_row,
    tree_rows,
    all_keys,
    all_values,
    adapter_down_input,
    low_out,
    resp_index,
    n_resp,
    prefix_rows,
):
    allowed = visible(resp_index, lengths_row, tree_rows, n_resp, prefix_rows)
    positions = jnp.arange(RESPONSE_TOKENS, dtype=jnp.int32)
    per_token_weight = jnp.where(
        positions < own_length,
        advantage / own_length.astype(jnp.float32),
        jnp.zeros((), jnp.float32),
    )
    output_cotangent = (per_token_weight[:, None] * output_grad.astype(jnp.float32)).astype(
        jnp.bfloat16
    )
    down_projected = jnp.dot(
        output_cotangent, low_out.T, preferred_element_type=jnp.float32
    ).astype(jnp.bfloat16)
    attention_cotangent = (
        per_token_weight[:, None] * attention_output_gradient.astype(jnp.float32)
        + adapter_scale
        * jnp.dot(down_projected, adapter_down_input, preferred_element_type=jnp.float32)
    ).astype(jnp.bfloat16)
    attention_result_rows, query_grad, key_grad, value_grad = attend_heads(
        queries, all_keys, all_values, allowed, attention_cotangent
    )
    projected_rows = jnp.dot(
        attention_result_rows, adapter_down_input.T, preferred_element_type=jnp.float32
    ).astype(jnp.bfloat16)
    input_gradient = adapter_scale * jnp.dot(
        down_projected.T, attention_result_rows, preferred_element_type=jnp.float32
    )
    output_gradient = adapter_scale * jnp.dot(
        projected_rows.T, output_cotangent, preferred_element_type=jnp.float32
    )
    adapter_grad = jnp.concatenate([input_gradient, output_gradient], axis=1)
    return (query_grad.astype(jnp.bfloat16), key_grad, value_grad, adapter_grad)


def adam_update_of(gradient, first_state, second_state, clip_factor):
    scaled = gradient * clip_factor
    moment = beta_first * first_state + (1.0 - beta_first) * scaled
    second_new = beta_second * second_state + (1.0 - beta_second) * scaled * scaled
    return moment / first_fix / (jnp.sqrt(second_new / second_fix) + adam_eps)


def on_device(
    queries,
    resp_keys,
    response_values,
    rotated_prompt_keys,
    prompt_value_rows,
    attention_output_gradient,
    output_grad,
    advantages,
    lengths,
    tree_mask,
    adapter,
    first_moment,
    second_moment,
):
    n_resp = lax.axis_size("resp")
    resp_index = lax.axis_index("resp")
    split = QUERY_HEADS * HEAD_SIZE
    whole = lax.all_gather(adapter.astype(jnp.bfloat16), "fsdp", axis=1, tiled=True)
    prompt_key_all, prompt_value_all, resp_key_all, resp_value_all = (
        lax.all_gather(rotated_prompt_keys, "resp", axis=1, tiled=True),
        lax.all_gather(prompt_value_rows, "resp", axis=1, tiled=True),
        lax.all_gather(resp_keys, "resp", axis=1, tiled=True),
        lax.all_gather(response_values, "resp", axis=1, tiled=True),
    )
    prefix_rows = prompt_key_all.shape[1]
    all_keys = jnp.concatenate([prompt_key_all[0], resp_key_all[0]], axis=0)
    all_values = jnp.concatenate([prompt_value_all[0], resp_value_all[0]], axis=0)
    per_resp = RESPONSE_TOKENS // BLK
    tree_rows = lax.dynamic_slice_in_dim(tree_mask[0], resp_index * per_resp, per_resp, 0)
    own_length = lax.dynamic_index_in_dim(lengths[0], resp_index, 0, keepdims=False)
    query_grad, key_grad, value_grad, adapter_grad = local_pass(
        queries[0],
        attention_output_gradient[0],
        output_grad[0],
        advantages[0, 0],
        own_length,
        lengths[0],
        tree_rows,
        all_keys,
        all_values,
        whole[:, :split],
        whole[:, split:],
        resp_index,
        n_resp,
        prefix_rows,
    )
    prompt_key_sum, prompt_value_sum, key_sum, value_sum = (
        lax.psum_scatter(
            key_grad[:prefix_rows].astype(jnp.bfloat16), "resp", scatter_dimension=0, tiled=True
        ).astype(jnp.float32),
        lax.psum_scatter(
            value_grad[:prefix_rows].astype(jnp.bfloat16), "resp", scatter_dimension=0, tiled=True
        ).astype(jnp.float32),
        lax.psum_scatter(
            key_grad[prefix_rows:].astype(jnp.bfloat16), "resp", scatter_dimension=0, tiled=True
        ).astype(jnp.float32),
        lax.psum_scatter(
            value_grad[prefix_rows:].astype(jnp.bfloat16), "resp", scatter_dimension=0, tiled=True
        ).astype(jnp.float32),
    )
    group_total = lax.psum(adapter_grad.astype(jnp.bfloat16), "resp").astype(jnp.float32)
    owned = lax.psum_scatter(group_total, "fsdp", scatter_dimension=1, tiled=True)
    squares = lax.psum(jnp.sum(owned * owned), "fsdp")
    clip_factor = max_norm / jnp.maximum(jnp.sqrt(squares), max_norm)
    update = adam_update_of(owned, first_moment, second_moment, clip_factor)
    return (
        query_grad[None],
        key_sum.astype(jnp.bfloat16)[None],
        value_sum.astype(jnp.bfloat16)[None],
        prompt_key_sum.astype(jnp.bfloat16)[None],
        prompt_value_sum.astype(jnp.bfloat16)[None],
        update,
    )


def solution(mesh):
    in_specs = (
        P("fsdp", "resp", None),
        P("fsdp", "resp", None),
        P("fsdp", "resp", None),
        P("fsdp", "resp", None),
        P("fsdp", "resp", None),
        P("fsdp", "resp", None),
        P("fsdp", "resp", None),
        P("fsdp", "resp"),
        P("fsdp", None),
        P("fsdp", None, None),
        P(None, "fsdp"),
        P(None, "fsdp"),
        P(None, "fsdp"),
    )
    out_specs = (
        P("fsdp", "resp", None),
        P("fsdp", "resp", None),
        P("fsdp", "resp", None),
        P("fsdp", "resp", None),
        P("fsdp", "resp", None),
        P(None, "fsdp"),
    )
    return jax.shard_map(
        on_device, mesh=mesh, in_specs=in_specs, out_specs=out_specs, check_vma=False
    )
```

profile of v0, /device:TPU:1, one launch (start us, length us, event | category | flops | bytes accessed | tf_op | source)
XLA Modules:
  0.0 620.6 jit_solution(5655002268369972522)
XLA Ops:
  14.7 51.6 %all-gather = bf16[64,120,16]{1,2,0:T(8,128)(2,1)S(1)} all-gather(bf16[1,120,16]{1,2,0:T(8,128)(2,1)S(1)} %convert_bitcast_fusion), channel_id=1, replica_groups=mesh['resp'=8,'fsdp'=64] {'fsdp'}, dimensions={0}, use_global_device_ids=true | all-gather | bytes 249600 | tf_op jit(solution)/shard_map/all_gather | solution.py:175
  66.8 1.9 convolution_convert_fusion.8
  72.2 20.9 %all_gather.15 = bf16[1,128,512]{2,1,0:T(8,128)(2,1)S(1)} all-gather(bf16[1,16,512]{2,1,0:T(8,128)(2,1)S(1)} %copy-done.49), channel_id=1, replica_groups=mesh['resp'=8,'fsdp'=64] {'resp'}, dimensions={1}, use_global_device_ids=true | all-gather | bytes 147456 | tf_op jit(solution)/shard_map/all_gather | solution.py:177
  93.1 18.8 %all_gather.17 = bf16[1,128,512]{2,1,0:T(8,128)(2,1)S(1)} all-gather(bf16[1,16,512]{2,1,0:T(8,128)(2,1)S(1)} %copy-done.50), channel_id=1, replica_groups=mesh['resp'=8,'fsdp'=64] {'resp'}, dimensions={1}, use_global_device_ids=true | all-gather | bytes 147456 | tf_op jit(solution)/shard_map/all_gather | solution.py:178
  112.8 1.6 fusion.107
  114.8 1.6 copy-done.5
  118.1 2.5 multiply_reduce_fusion.3
  120.5 1.3 convolution_bitcast_fusion.7
  124.2 1.3 multiply_reduce_fusion
  129.0 1.3 multiply_reduce_fusion.1
  130.3 1.3 multiply_reduce_fusion.2
  131.7 2.9 fusion
  134.5 1.4 fusion.23
  136.0 2.9 fusion.27
  145.5 1.9 fusion.25
  150.7 3.1 convolution_bitcast_fusion.5
  156.1 1.3 maximum_convert_fusion
  157.6 1.3 copy.202
  160.2 2.4 copy.204
  165.2 1.9 convolution_convert_fusion.6
  167.9 1.8 convolution_convert_fusion.4
  169.9 54.1 %all-reduce.5.cloned.1.call-done = bf16[16,7680]{1,0:T(8,128)(2,1)} async-done(((bf16[16,7680]{1,0:T(8,128)(2,1)}), bf16[16,7680]{1,0:T(8,128)(2,1)}) %all-reduce.5.cloned.1.call-update) | async-done | bytes 245776 | tf_op jit(solution)/shard_map/psum | solution.py:218
  224.0 250.4 %all-reduce.6 = f32[16,7680]{1,0:T(8,128)S(1)} all-reduce(bf16[16,7680]{1,0:T(8,128)(2,1)} %all-reduce.5.cloned.1.call-done), channel_id=6, replica_groups=mesh['resp'=8,'fsdp'=64] {'fsdp'}, use_global_device_ids=true, to_apply=%region_17.18.clone | all-reduce | flops 122880 | bytes 737280
  476.0 129.7 %psum.15 = f32[]{:T(128)} all-reduce(f32[]{:T(128)} %multiply_reduce_fusion.4), channel_id=1, replica_groups=mesh['resp'=8,'fsdp'=64] {'fsdp'}, use_global_device_ids=true, to_apply=%region_19.20 | all-reduce | flops 1 | bytes 8 | tf_op jit(solution)/shard_map/psum | solution.py:220
  (198 shorter events, 43.7 us)
Async XLA Ops:
  7.2 61.5 %copy-start.45 = (bf16[1,128,2560]{2,1,0:T(8,128)(2,1)S(1)}, bf16[1,128,2560]{2,1,0:T(8,128)(2,1)}, u32[]{:S(2)}) copy-start(bf16[1,128,2560]{2,1,0:T(8,128)(2,1)} %param.18) | copy-start | bytes 1966084
  7.2 105.6 %all-gather.4.cloned.1.call-start = ((), (), s32[]{:S(2)}) async-start(), calls=%async_computation.4 | async-start | bytes 1179648 | tf_op jit(solution)/shard_map/all_gather | solution.py:179
  7.9 109.2 %all-gather.6.cloned.1.call-start = ((), (), s32[]{:S(2)}) async-start(), calls=%async_computation.5 | async-start | bytes 1179648 | tf_op jit(solution)/shard_map/all_gather | solution.py:180
  8.7 215.3 %all-reduce.5.cloned.1.call-start = ((), (), s32[]{:S(2)}) async-start(), calls=%async_computation.6 | async-start | bytes 491520 | tf_op jit(solution)/shard_map/psum | solution.py:218
  12.0 57.1 %copy-start.53 = (f32[128]{0:T(128)}, f32[128]{0:T(128)S(1)}, u32[]{:S(2)}) copy-start(f32[128]{0:T(128)S(1)} %compare_select_fusion) | copy-start | bytes 1540
  69.1 24.0 %copy-start.50 = (bf16[1,16,512]{2,1,0:T(8,128)(2,1)S(1)}, bf16[1,16,512]{2,1,0:T(8,128)(2,1)}, u32[]{:S(2)}) copy-start(bf16[1,16,512]{2,1,0:T(8,128)(2,1)} %param.17) | copy-start | bytes 49156
  70.2 54.0 %copy-start.31 = (bf16[128,640]{0,1:T(8,128)(2,1)}, bf16[128,640]{0,1:T(8,128)(2,1)S(1)}, u32[]{:S(2)}) copy-start(bf16[128,640]{0,1:T(8,128)(2,1)S(1)} %copy.140) | copy-start | bytes 491524
  114.3 6.2 copy-start.2
  118.0 6.1 copy-start.16
  131.7 4.3 copy-start.17
  136.0 4.0 copy-start.3
  136.0 4.0 copy-start.9
  139.5 9.7 %copy-start.25 = (bf16[1152,128]{0,1:T(8,128)(2,1)}, bf16[1152,128]{0,1:T(8,128)(2,1)S(1)}, u32[]{:S(2)}) copy-start(bf16[1152,128]{0,1:T(8,128)(2,1)S(1)} %convolution_bitcast_fusion.8) | copy-start | bytes 884740
  145.2 461.9 %reduce-scatter.18.cloned.1.call-start = ((), (), s32[]{:S(2)}) async-start(), calls=%async_computation.9 | async-start | bytes 147456
  145.5 4.4 copy-start.26
  145.5 4.4 copy-start.27
  153.8 454.8 %reduce-scatter.20.cloned.1.call-start = ((), (), s32[]{:S(2)}) async-start(), calls=%async_computation.10 | async-start | bytes 147456
  156.0 454.2 %reduce-scatter.14.cloned.1.call-start = ((), (), s32[]{:S(2)}) async-start(), calls=%async_computation.7 | async-start | bytes 1179648
  158.9 453.1 %reduce-scatter.16.cloned.1.call-start = ((), (), s32[]{:S(2)}) async-start(), calls=%async_computation.8 | async-start | bytes 1179648
  159.1 5.4 copy-start.11
  159.1 5.4 copy-start.30
  160.2 5.0 copy-start.7
  167.9 438.5 %copy-start.51 = (f32[16,120]{1,0:T(8,128)S(1)}, f32[16,120]{1,0:T(8,128)}, u32[]{:S(2)}) copy-start(f32[16,120]{1,0:T(8,128)} %param.25) | copy-start | bytes 23044
  167.9 438.5 %copy-start.52 = (f32[16,120]{1,0:T(8,128)S(1)}, f32[16,120]{1,0:T(8,128)}, u32[]{:S(2)}) copy-start(f32[16,120]{1,0:T(8,128)} %param.24) | copy-start | bytes 23044
  (38 other events, 70.7 us)
Sparse Core Ops, SparseCore 0:
  10.1 41.7 all-gather.3
  53.9 40.0 all-gather.5
  145.3 78.6 all-reduce.4
  227.4 37.3 reduce-scatter.17
  268.0 37.7 reduce-scatter.19
  308.8 40.8 reduce-scatter.13
  352.7 40.0 reduce-scatter.15
where the time goes:
time: 622 us; the launch traced here: 621 us
  blocking collectives  471 us (76%)
  waiting for transfers between devices  55.5 us (9%)
  matrix products  37.4 us (6%)
  local copies, waits for them, and re-layouts  27.4 us (4%)
  between operations  17.7 us (3%)
  other arithmetic  10.7 us (2%)
    unnamed x1, blocking collectives  250 us
    psum x1, blocking collectives, on_device(): squares = lax.psum(jnp.sum(owned * owned), 'fsdp')  130 us
    psum x1, waiting for transfers between devices, on_device(): lax.psum(adapter_grad.astype(jnp.bfloat16), 'resp').astype(jnp.float32)  54.1 us
    all_gather x1, blocking collectives, on_device(): lax.all_gather(adapter.astype(jnp.bfloat16), 'fsdp', axis=1, tiled=True)  51.6 us
    all_gather x1, blocking collectives, on_device(): lax.all_gather(rotated_prompt_keys, 'resp', axis=1, tiled=True)  20.9 us
    unnamed x126, local copies, waits for them, and re-layouts  20.5 us
    all_gather x1, blocking collectives, on_device(): lax.all_gather(prompt_value_rows, 'resp', axis=1, tiled=True)  18.8 us
  transfers between devices with their start and end apart: 7, of which 1 were waited for; matrix products, arithmetic and copies ran while one was open for 7% of the time, Pallas kernels for 0%

commit v1 on v0

v1 whole, which is shorter than its diff:
```python
import functools

import jax
import jax.numpy as jnp
from jax import lax
from jax.experimental import pallas as pl
from jax.experimental.pallas import tpu as pltpu
from jax.sharding import PartitionSpec as P

HEAD = 128
Q_HEADS = 20
KV_HEADS = 4
MEMBERS = Q_HEADS // KV_HEADS
BLK = 64
JOIN = 4
TOK = 128
PRE = 16
RANK = 16
LANES = 128

adapter_scale = 2.0
max_norm = 1.0
beta_first = 0.9
beta_second = 0.999
first_fix = 0.9999734386011124
second_fix = 0.0952078516
adam_eps = 1e-08

SCALE = HEAD ** (-0.5)
LOG2E = 1.4426950408889634
HIDDEN = -1e30

NT = (((1,), (1,)), ((), ()))
NN = (((1,), (0,)), ((), ()))
TN = (((0,), (0,)), ((), ()))


def dot(a, b, dims):
    return lax.dot_general(a, b, dims, preferred_element_type=jnp.float32)


def token_column(place_ref, lengths_ref, adv_ref):
    own = lengths_ref[0, place_ref[0]]
    weight = adv_ref[0, 0] / own.astype(jnp.float32)
    pos = lax.broadcasted_iota(jnp.int32, (TOK, LANES), 0)
    return jnp.where(pos < own, weight, 0.0)[:, :1]


def rows_of(i, size):
    return pl.ds(pl.multiple_of(i * size, size), size)


def block_rows(b2):
    per = TOK // BLK
    return pl.ds(pl.multiple_of((b2 // per) * (TOK + PRE) + PRE + (b2 % per) * BLK, PRE), BLK)


def block_bias(b2, r, lengths_ref, tree_ref):
    per = TOK // BLK
    r2 = b2 // per
    key_pos = (b2 % per) * BLK + lax.broadcasted_iota(jnp.int32, (BLK, TOK), 0)
    query_pos = lax.broadcasted_iota(jnp.int32, (BLK, TOK), 1)
    bit = jnp.where(query_pos < BLK, tree_ref[per * r, b2], tree_ref[per * r + 1, b2])
    reach = jnp.where(r2 == r, query_pos, TOK)
    seen = (bit == 1) & (key_pos < lengths_ref[0, r2]) & (key_pos <= reach)
    return jnp.where(seen, 0.0, HIDDEN)


def prepare_kernel(
    place_ref, lengths_ref, tree_ref, adv_ref, parts_ref, q_ref, og_ref, ag_ref,
    out_cot_ref, low_t_ref, low_in_ref, qs_ref, gs_ref, gt_ref, list_ref, bias_ref,
    whole_ref,
):
    n, _, _ = parts_ref.shape
    width = whole_ref.shape[1] // n
    for i in range(n):
        whole_ref[:, i * width : (i + 1) * width] = parts_ref[i, :, :width].astype(jnp.float32)
    split = ag_ref.shape[1]
    weight = token_column(place_ref, lengths_ref, adv_ref)
    out_cot_ref[...] = (weight * og_ref[...].astype(jnp.float32)).astype(jnp.bfloat16)
    low_in_ref[...] = whole_ref[:, :split].astype(jnp.bfloat16)
    low_out = whole_ref[:, split:].astype(jnp.bfloat16)
    low_t = dot(low_out, out_cot_ref[...], NT).astype(jnp.bfloat16)
    low_t_ref[...] = low_t
    for i in range(Q_HEADS):
        part = slice(i * HEAD, (i + 1) * HEAD)
        rows = slice(i * TOK, (i + 1) * TOK)
        added = adapter_scale * dot(low_t, low_in_ref[:, part], TN)
        grad = (weight * ag_ref[:, part].astype(jnp.float32) + added).astype(jnp.bfloat16)
        gs_ref[rows, :] = grad
        gt_ref[:, rows] = jnp.transpose(grad.astype(jnp.float32)).astype(jnp.bfloat16)
        qs_ref[rows, :] = q_ref[:, part]

    r = place_ref[0]
    per = TOK // BLK
    n_blocks = tree_ref.shape[1]
    first = n_blocks // per * PRE // BLK
    bias_ref[: first * BLK, :] = jnp.zeros((first * BLK, TOK), jnp.float32)

    def step(b2, count):
        bits = tree_ref[per * r, b2] + tree_ref[per * r + 1, b2]
        seen = (bits > 0) & ((b2 % per) * BLK < lengths_ref[0, b2 // per])

        @pl.when(seen)
        def _():
            list_ref[2 + count - first] = b2
            bias_ref[rows_of(count, BLK), :] = block_bias(b2, r, lengths_ref, tree_ref)

        return count + jnp.where(seen, 1, 0)

    count = lax.fori_loop(0, n_blocks, step, first)
    steps = (count + JOIN - 1) // JOIN
    list_ref[0] = count
    list_ref[1] = steps

    def hide(i, carry):
        bias_ref[rows_of(i, BLK), :] = jnp.full((BLK, TOK), HIDDEN, jnp.float32)
        return carry

    lax.fori_loop(count, steps * JOIN, hide, 0)


def places_of(n_blocks):
    places = n_blocks + n_blocks // (TOK // BLK) * PRE // BLK
    return -(-places // JOIN) * JOIN


def prepare(place, lengths, tree, advantages, parts, q, og, ag):
    smem = pl.BlockSpec(memory_space=pltpu.SMEM)
    vmem = pl.BlockSpec(memory_space=pltpu.VMEM)
    split = ag.shape[1]
    wide = split + og.shape[1]
    n_blocks = tree.shape[1]
    return pl.pallas_call(
        prepare_kernel,
        out_shape=(
            jax.ShapeDtypeStruct(og.shape, jnp.bfloat16),
            jax.ShapeDtypeStruct((RANK, TOK), jnp.bfloat16),
            jax.ShapeDtypeStruct((RANK, split), jnp.bfloat16),
            jax.ShapeDtypeStruct((split, HEAD), jnp.bfloat16),
            jax.ShapeDtypeStruct((split, HEAD), jnp.bfloat16),
            jax.ShapeDtypeStruct((HEAD, split), jnp.bfloat16),
            jax.ShapeDtypeStruct((n_blocks + 2,), jnp.int32),
            jax.ShapeDtypeStruct((places_of(n_blocks) * BLK, TOK), jnp.float32),
        ),
        in_specs=[smem] * 4 + [vmem] * 4,
        out_specs=[vmem] * 6 + [smem, vmem],
        scratch_shapes=[pltpu.VMEM((RANK, wide), jnp.float32)],
        compiler_params=pltpu.CompilerParams(vmem_limit_bytes=16 * 1024 * 1024),
        cost_estimate=pl.CostEstimate(flops=80_000_000, bytes_accessed=6_000_000, transcendentals=0),
        name="prepare",
    )(place, lengths, tree, advantages, parts, q, og, ag)


def spread(bias):
    return jnp.concatenate([bias] * MEMBERS, axis=1)


def fold(x, op):
    return op(x.reshape(x.shape[0] // 8, 8, x.shape[1]), axis=0)


def attend_kernel(
    list_ref, bias_hbm, qs_hbm, gs_hbm, gt_hbm, kv_ref,
    out_ref, turned_ref, kv_grad_ref,
    bias_ref, qs_ref, gs_ref, gt_ref, keys_ref, score_ref, acc_ref, peak_ref, total_ref, inner_ref,
    sums_ref, zero_ref,
    in_sem, place_sem, prompt_in_sem, prompt_sem, block_sem,
):
    c = SCALE * LOG2E
    n_blocks = block_sem.shape[0]
    n_resp = prompt_sem.shape[0]
    first = n_resp * PRE // BLK
    group = MEMBERS * TOK
    v0 = KV_HEADS * HEAD
    width = JOIN * BLK
    count = list_ref[0]
    steps = list_ref[1]

    def load(src, dst, i):
        return pltpu.make_async_copy(src, dst, in_sem.at[i])

    load_q, load_bias, load_g, load_gt = (
        load(qs_hbm, qs_ref, 0), load(bias_hbm, bias_ref, 1), load(gs_hbm, gs_ref, 2), load(gt_hbm, gt_ref, 3)
    )
    prompt_in = [
        pltpu.make_async_copy(
            kv_ref.at[pl.ds(i * (TOK + PRE), PRE)], keys_ref.at[pl.ds(i * PRE, PRE)], prompt_in_sem.at[i]
        )
        for i in range(n_resp)
    ]

    def bring(i):
        b2 = list_ref[2 + i - first]
        return pltpu.make_async_copy(kv_ref.at[block_rows(b2)], keys_ref.at[rows_of(i, BLK)], place_sem.at[i])

    def start(i, carry):
        bring(i).start()
        return carry

    for copy in prompt_in:
        copy.start()
    load_q.start()
    lax.fori_loop(first, count, start, 0)
    load_bias.start()
    load_g.start()
    load_gt.start()

    zero_ref[...] = jnp.zeros_like(zero_ref)
    peak_ref[...] = jnp.full_like(peak_ref, HIDDEN)
    total_ref[...] = jnp.zeros_like(total_ref)
    acc_ref[...] = jnp.zeros_like(acc_ref)

    def blank(i, carry):
        keys_ref[rows_of(i, BLK), :] = jnp.zeros((BLK, keys_ref.shape[1]), jnp.bfloat16)
        return carry

    lax.fori_loop(count, steps * JOIN, blank, 0)

    def block_out(src, b2):
        return pltpu.make_async_copy(src, kv_grad_ref.at[block_rows(b2)], block_sem.at[b2])

    def unseen(b2, at):
        hit = (at < count) & (list_ref[jnp.minimum(2 + at - first, n_blocks + 1)] == b2)

        @pl.when(jnp.logical_not(hit))
        def _():
            block_out(zero_ref, b2).start()

        return at + jnp.where(hit, 1, 0)

    lax.fori_loop(0, n_blocks, unseen, first)
    for copy in prompt_in:
        copy.wait()
    load_q.wait()
    load_bias.wait()

    def cols(h):
        return slice(h * group, (h + 1) * group)

    def score_step(i, carry):
        def arrive(at, carry):
            bring(at).wait()
            return carry

        lax.fori_loop(jnp.maximum(i * JOIN, first), jnp.minimum((i + 1) * JOIN, count), arrive, 0)
        rows = rows_of(i, width)
        bias = spread(bias_ref[rows, :])
        for h in range(KV_HEADS):
            s = dot(keys_ref[rows, h * HEAD : (h + 1) * HEAD], qs_ref[cols(h), :], NT) + bias
            score_ref[rows, cols(h)] = s
            peak_ref[:, cols(h)] = jnp.maximum(peak_ref[:, cols(h)], fold(s, jnp.max))
        return carry

    lax.fori_loop(0, steps, score_step, 0)
    peak = jnp.max(peak_ref[...], axis=0, keepdims=True) * c
    peak_ref[...] = jnp.broadcast_to(peak, peak_ref.shape)

    def value_step(i, carry):
        rows = rows_of(i, width)
        for h in range(KV_HEADS):
            e = jnp.exp2(score_ref[rows, cols(h)] * c - peak_ref[:1, cols(h)])
            score_ref[rows, cols(h)] = e
            total_ref[:, cols(h)] += fold(e, jnp.sum)
            v = keys_ref[rows, v0 + h * HEAD : v0 + (h + 1) * HEAD]
            acc_ref[:, cols(h)] += dot(v, e.astype(jnp.bfloat16), TN)
        return carry

    lax.fori_loop(0, steps, value_step, 0)
    inverse = 1.0 / jnp.sum(total_ref[...], axis=0, keepdims=True)
    total_ref[...] = jnp.broadcast_to(inverse, total_ref.shape)
    load_g.wait()
    load_gt.wait()
    for i in range(Q_HEADS):
        part = slice(i * TOK, (i + 1) * TOK)
        rounded = (acc_ref[:, part] * inverse[:, part]).astype(jnp.bfloat16)
        out_ref[:, part] = rounded
        across = gt_ref[:, part].astype(jnp.float32) * rounded.astype(jnp.float32)
        inner_ref[:, part] = jnp.broadcast_to(jnp.sum(across, axis=0, keepdims=True), (8, TOK))
    acc_ref[...] = jnp.zeros_like(acc_ref)

    def back_step(i, carry):
        rows = rows_of(i, width)
        for h in range(KV_HEADS):
            kc = slice(h * HEAD, (h + 1) * HEAD)
            vc = slice(v0 + h * HEAD, v0 + (h + 1) * HEAD)
            w = score_ref[rows, cols(h)] * total_ref[:1, cols(h)]
            across = dot(keys_ref[rows, vc], gs_ref[cols(h), :], NT)
            sums_ref[rows, vc] = dot(w.astype(jnp.bfloat16), gs_ref[cols(h), :], NN).astype(jnp.bfloat16)
            ds = (w * (across - inner_ref[:1, cols(h)])).astype(jnp.bfloat16)
            sums_ref[rows, kc] = (dot(ds, qs_ref[cols(h), :], NN) * SCALE).astype(jnp.bfloat16)
            acc_ref[:, cols(h)] += dot(keys_ref[rows, kc], ds, TN)

        def send(at, carry):
            block_out(sums_ref.at[rows_of(at, BLK)], list_ref[2 + at - first]).start()
            return carry

        lax.fori_loop(jnp.maximum(i * JOIN, first), jnp.minimum((i + 1) * JOIN, count), send, 0)
        return carry

    lax.fori_loop(0, steps, back_step, 0)
    prompts = [
        pltpu.make_async_copy(
            sums_ref.at[pl.ds(i * PRE, PRE)], kv_grad_ref.at[pl.ds(i * (TOK + PRE), PRE)], prompt_sem.at[i]
        )
        for i in range(n_resp)
    ]
    for copy in prompts:
        copy.start()
    turned_ref[...] = (acc_ref[...] * SCALE).astype(jnp.bfloat16)
    for copy in prompts:
        copy.wait()

    def finished(b2, carry):
        block_out(zero_ref, b2).wait()
        return carry

    lax.fori_loop(0, n_blocks, finished, 0)


def attend(blocks, bias, qs, gs, gt, kv, n_resp):
    smem = pl.BlockSpec(memory_space=pltpu.SMEM)
    vmem = pl.BlockSpec(memory_space=pltpu.VMEM)
    hbm = pl.BlockSpec(memory_space=pl.ANY)
    split = qs.shape[0]
    rows, columns = bias.shape[0], kv.shape[1]
    return pl.pallas_call(
        attend_kernel,
        out_shape=(
            jax.ShapeDtypeStruct((HEAD, split), jnp.bfloat16),
            jax.ShapeDtypeStruct((HEAD, split), jnp.bfloat16),
            jax.ShapeDtypeStruct(kv.shape, jnp.bfloat16),
        ),
        in_specs=[smem] + [hbm] * 5,
        out_specs=[vmem, vmem, hbm],
        scratch_shapes=[
            pltpu.VMEM(bias.shape, jnp.float32),
            pltpu.VMEM(qs.shape, jnp.bfloat16),
            pltpu.VMEM(gs.shape, jnp.bfloat16),
            pltpu.VMEM(gt.shape, jnp.bfloat16),
            pltpu.VMEM((rows, columns), jnp.bfloat16),
            pltpu.VMEM((rows, split), jnp.float32),
            pltpu.VMEM((HEAD, split), jnp.float32),
            pltpu.VMEM((8, split), jnp.float32),
            pltpu.VMEM((8, split), jnp.float32),
            pltpu.VMEM((8, split), jnp.float32),
            pltpu.VMEM((rows, columns), jnp.bfloat16),
            pltpu.VMEM((BLK, columns), jnp.bfloat16),
            pltpu.SemaphoreType.DMA((4,)),
            pltpu.SemaphoreType.DMA((rows // BLK,)),
            pltpu.SemaphoreType.DMA((n_resp,)),
            pltpu.SemaphoreType.DMA((n_resp,)),
            pltpu.SemaphoreType.DMA((n_resp * (TOK // BLK),)),
        ],
        compiler_params=pltpu.CompilerParams(vmem_limit_bytes=56 * 1024 * 1024),
        cost_estimate=pl.CostEstimate(
            flops=3_800_000_000, bytes_accessed=8_000_000, transcendentals=3_000_000
        ),
        name="attend",
    )(blocks, bias, qs, gs, gt, kv)


def pieces_kernel(out_t_ref, low_t_ref, low_in_ref, out_cot_ref, parts_ref, wide_ref):
    projected_t = jnp.zeros((RANK, TOK), jnp.float32)
    for i in range(Q_HEADS):
        part = slice(i * TOK, (i + 1) * TOK)
        projected_t += dot(low_in_ref[:, part], out_t_ref[:, part], NN)
        wide_ref[:, part] = adapter_scale * dot(low_t_ref[...], out_t_ref[:, part], NT)
    split = out_t_ref.shape[1]
    wide_ref[:, split:] = adapter_scale * dot(projected_t.astype(jnp.bfloat16), out_cot_ref[...], NN)
    parts_ref[...] = jnp.zeros_like(parts_ref)
    n_parts = parts_ref.shape[0]
    piece = wide_ref.shape[1] // n_parts
    for i in range(n_parts):
        parts_ref[i, :, :piece] = wide_ref[:, i * piece : (i + 1) * piece].astype(jnp.bfloat16)


PIECES_FLOPS = 200_000_000_000


def pieces(out_t, low_t, low_in, out_cot, n_fsdp):
    vmem = pl.BlockSpec(memory_space=pltpu.VMEM)
    wide = out_t.shape[1] + out_cot.shape[1]
    return pl.pallas_call(
        pieces_kernel,
        out_shape=jax.ShapeDtypeStruct((n_fsdp, RANK, LANES), jnp.bfloat16),
        in_specs=[vmem] * 4,
        out_specs=vmem,
        scratch_shapes=[pltpu.VMEM((RANK, wide), jnp.float32)],
        cost_estimate=pl.CostEstimate(flops=PIECES_FLOPS, bytes_accessed=2_500_000, transcendentals=0),
        name="pieces",
    )(out_t, low_t, low_in, out_cot)


def turn_kernel(turned_ref, out_ref):
    for i in range(Q_HEADS):
        part = slice(i * TOK, (i + 1) * TOK)
        out_ref[:, part] = jnp.transpose(turned_ref[:, part].astype(jnp.float32)).astype(jnp.bfloat16)


def turn(turned):
    vmem = pl.BlockSpec(memory_space=pltpu.VMEM)
    return pl.pallas_call(
        turn_kernel,
        out_shape=jax.ShapeDtypeStruct((TOK, turned.shape[1]), jnp.bfloat16),
        in_specs=[vmem],
        out_specs=vmem,
        cost_estimate=pl.CostEstimate(flops=1_000_000, bytes_accessed=1_300_000, transcendentals=0),
        name="turn",
    )(turned)


def pack_kernel(rk_ref, rv_ref, pk_ref, pv_ref, own_ref):
    half = rk_ref.shape[2]
    own_ref[:PRE, :half] = pk_ref[0]
    own_ref[:PRE, half:] = pv_ref[0]
    own_ref[PRE:, :half] = rk_ref[0]
    own_ref[PRE:, half:] = rv_ref[0]


def pack(rk, rv, pk, pv):
    vmem = pl.BlockSpec(memory_space=pltpu.VMEM)
    return pl.pallas_call(
        pack_kernel,
        out_shape=jax.ShapeDtypeStruct((PRE + rk.shape[1], 2 * rk.shape[2]), jnp.bfloat16),
        in_specs=[vmem] * 4,
        out_specs=vmem,
        cost_estimate=pl.CostEstimate(flops=1_000, bytes_accessed=600_000, transcendentals=0),
        name="pack",
    )(rk, rv, pk, pv)


def shards_kernel(adapter_ref, parts_ref):
    width = adapter_ref.shape[1]
    parts_ref[0] = jnp.zeros(parts_ref.shape[1:], jnp.bfloat16)
    parts_ref[0, :, :width] = adapter_ref[...].astype(jnp.bfloat16)
    shard = parts_ref[0]
    for i in range(1, parts_ref.shape[0]):
        parts_ref[i] = shard


def shards(adapter, n_fsdp):
    vmem = pl.BlockSpec(memory_space=pltpu.VMEM)
    return pl.pallas_call(
        shards_kernel,
        out_shape=jax.ShapeDtypeStruct((n_fsdp, RANK, LANES), jnp.bfloat16),
        in_specs=[vmem],
        out_specs=vmem,
        cost_estimate=pl.CostEstimate(flops=1_000, bytes_accessed=300_000, transcendentals=0),
        name="shards",
    )(adapter)


def group_sum_kernel(parts_ref, copies_ref):
    total = jnp.sum(parts_ref[...].astype(jnp.float32), axis=0)
    for i in range(copies_ref.shape[0]):
        copies_ref[i] = total


def group_sum(parts, copies):
    vmem = pl.BlockSpec(memory_space=pltpu.VMEM)
    return pl.pallas_call(
        group_sum_kernel,
        out_shape=jax.ShapeDtypeStruct((copies,) + parts.shape[1:], jnp.float32),
        in_specs=[vmem],
        out_specs=vmem,
        cost_estimate=pl.CostEstimate(flops=200_000, bytes_accessed=400_000, transcendentals=0),
        name="group_sum",
    )(parts)


def norm_kernel(parts_ref, owned_ref, squares_ref):
    owned = jnp.sum(parts_ref[...], axis=0)
    owned_ref[...] = owned
    squares = jnp.sum(jnp.sum(owned * owned, axis=0, keepdims=True), axis=1, keepdims=True)
    squares_ref[...] = jnp.broadcast_to(squares[None], squares_ref.shape)


def norm(parts, copies):
    vmem = pl.BlockSpec(memory_space=pltpu.VMEM)
    return pl.pallas_call(
        norm_kernel,
        out_shape=(
            jax.ShapeDtypeStruct(parts.shape[1:], jnp.float32),
            jax.ShapeDtypeStruct((copies, 1, LANES), jnp.float32),
        ),
        in_specs=[vmem],
        out_specs=[vmem] * 2,
        cost_estimate=pl.CostEstimate(flops=100_000, bytes_accessed=100_000, transcendentals=0),
        name="norm",
    )(parts)


def finish_kernel(
    kv_ref, owned_ref, squares_ref, first_ref, second_ref,
    rk_ref, rv_ref, pk_ref, pv_ref, update_ref,
):
    half = rk_ref.shape[2]
    rk_ref[0] = kv_ref[PRE:, :half]
    rv_ref[0] = kv_ref[PRE:, half:]
    pk_ref[0] = kv_ref[:PRE, :half]
    pv_ref[0] = kv_ref[:PRE, half:]
    width = first_ref.shape[1]
    squares = jnp.sum(squares_ref[...], axis=0)[:, :width]
    clip_factor = max_norm / jnp.maximum(jnp.sqrt(squares), max_norm)
    scaled = owned_ref[:, :width] * clip_factor
    moment = beta_first * first_ref[...] + (1.0 - beta_first) * scaled
    second_new = beta_second * second_ref[...] + (1.0 - beta_second) * scaled * scaled
    update_ref[...] = moment / first_fix / (jnp.sqrt(second_new / second_fix) + adam_eps)


def finish(kv_sum, owned, squares, first, second):
    vmem = pl.BlockSpec(memory_space=pltpu.VMEM)
    half = kv_sum.shape[1] // 2
    return pl.pallas_call(
        finish_kernel,
        out_shape=(
            jax.ShapeDtypeStruct((1, TOK, half), jnp.bfloat16),
            jax.ShapeDtypeStruct((1, TOK, half), jnp.bfloat16),
            jax.ShapeDtypeStruct((1, PRE, half), jnp.bfloat16),
            jax.ShapeDtypeStruct((1, PRE, half), jnp.bfloat16),
            jax.ShapeDtypeStruct(first.shape, jnp.float32),
        ),
        in_specs=[vmem] * 5,
        out_specs=[vmem] * 5,
        cost_estimate=pl.CostEstimate(flops=100_000, bytes_accessed=800_000, transcendentals=4_000),
        name="finish",
    )(kv_sum, owned, squares, first, second)


def swap(x, axis):
    return lax.all_to_all(x, axis, 0, 0, tiled=True)


def on_device(
    queries, resp_keys, response_values, rotated_prompt_keys, prompt_value_rows,
    attention_output_gradient, output_grad, advantages, lengths, tree_mask,
    adapter, first_moment, second_moment,
):
    n_resp = lax.axis_size("resp")
    n_fsdp = lax.axis_size("fsdp")
    place = lax.axis_index("resp").astype(jnp.int32).reshape(1)
    own_kv = pack(resp_keys, response_values, rotated_prompt_keys, prompt_value_rows)
    kv = lax.all_gather(own_kv, "resp", axis=0, tiled=True)
    gathered = swap(shards(adapter, n_fsdp), "fsdp")
    out_cot, low_t, low_in, qs, gs, gt, blocks, bias = prepare(
        place, lengths, tree_mask[0], advantages, gathered, queries[0], output_grad[0],
        attention_output_gradient[0],
    )
    out_t, turned, kv_grad = attend(blocks, bias, qs, gs, gt, kv, n_resp)
    kv_sum = lax.psum_scatter(kv_grad, "resp", scatter_dimension=0, tiled=True)
    arrived = swap(pieces(out_t, low_t, low_in, out_cot, n_fsdp), "fsdp")
    q_grad = turn(turned)
    arrived, q_grad = lax.optimization_barrier((arrived, q_grad))
    copies = group_sum(arrived, n_resp)
    owned, squares = norm(swap(copies, "resp"), n_fsdp)
    squares = swap(squares, "fsdp")
    key_sum, value_sum, prompt_key_sum, prompt_value_sum, update = finish(
        kv_sum, owned, squares, first_moment, second_moment
    )
    return (q_grad[None], key_sum, value_sum, prompt_key_sum, prompt_value_sum, update)


def solution(mesh):
    tokens = P("fsdp", "resp", None)
    columns = P(None, "fsdp")
    in_specs = (
        (tokens,) * 7
        + (P("fsdp", "resp"), P("fsdp", None), P("fsdp", None, None))
        + (columns,) * 3
    )
    out_specs = (tokens,) * 5 + (columns,)
    return jax.shard_map(
        on_device, mesh=mesh, in_specs=in_specs, out_specs=out_specs, check_vma=False
    )
```

time: 622 us -> 139 us (0.22)
  blocking collectives: 471 us -> 31.5 us
  matrix products: 37.4 us -> 0 us
  starting transfers between devices: 0.5 us -> 29.1 us
  waiting for transfers between devices: 55.5 us -> 27.7 us
  Pallas kernels: 0 us -> 25 us
  local copies, waits for them, and re-layouts: 27.4 us -> 10.5 us
  other arithmetic: 10.7 us -> 0 us
    unnamed x1 -> x0, blocking collectives: 250 us -> none
    psum x1 -> x0, blocking collectives: 130 us -> none  [on_device(): squares = lax.psum(jnp.sum(owned * owned), 'fsdp')]
    all_gather x3 -> x0, blocking collectives: 91.4 us -> none  [the longest x1 51.6 us: on_device(): lax.all_gather(adapter.astype(jnp.bfloat16), 'fsdp', axis=1, tiled=True)]
    psum x1 -> x0, waiting for transfers between devices: 54.1 us -> none  [on_device(): lax.psum(adapter_grad.astype(jnp.bfloat16), 'resp').astype(jnp.float32)]
    dot_general x28 -> x0, matrix products: 37.4 us -> none  [the longest x4 6.46 us: attend_heads(): jnp.einsum('gtk,kd->tgd', weight_half, value_head, preferred_element_type...]
    all_to_all x0 -> x2, blocking collectives: none -> 31.5 us  [swap(): return lax.all_to_all(x, axis, 0, 0, tiled=True)]
    all_to_all x0 -> x2, starting transfers between devices: none -> 29 us  [swap(): return lax.all_to_all(x, axis, 0, 0, tiled=True)]
    pallas_call x0 -> x9, Pallas kernels: none -> 25 us  [the longest x1 8.32 us: attend(): pl.pallas_call(attend_kernel, out_shape=(jax.ShapeDtypeStruct((HEAD, spli...]
  transfers between devices with their start and end apart: 7 -> 4, of which waited for: 1 -> 3; matrix products, arithmetic and copies ran while one was open for 7% -> 0% of each run, Pallas kernels for 0% -> 9%
where the time goes in v1:
time: 139 us
  blocking collectives  31.5 us (23%)
  starting transfers between devices  29.1 us (21%)
  waiting for transfers between devices  27.7 us (20%)
  Pallas kernels  25 us (18%)
  between operations  14.8 us (11%)
  local copies, waits for them, and re-layouts  10.5 us (8%)
    all_to_all x2, blocking collectives, swap(): return lax.all_to_all(x, axis, 0, 0, tiled=True)  31.5 us
    all_to_all x2, starting transfers between devices, swap(): return lax.all_to_all(x, axis, 0, 0, tiled=True)  29 us
    all_to_all x2, waiting for transfers between devices, swap(): return lax.all_to_all(x, axis, 0, 0, tiled=True)  21.1 us
    unnamed x28, local copies, waits for them, and re-layouts  10.5 us
    pallas_call x1, Pallas kernels, attend(): pl.pallas_call(attend_kernel, out_shape=(jax.ShapeDtypeStruct((HEAD, spli...  8.32 us
    all_gather x1, waiting for transfers between devices, on_device(): kv = lax.all_gather(own_kv, 'resp', axis=0, tiled=True)  6.55 us
    pallas_call x1, Pallas kernels, pieces(): pl.pallas_call(pieces_kernel, out_shape=jax.ShapeDtypeStruct((n_fsdp, RAN...  3.27 us
    pallas_call x1, Pallas kernels, prepare(): pl.pallas_call(prepare_kernel, out_shape=(jax.ShapeDtypeStruct(og.shape,...  3.04 us
  transfers between devices with their start and end apart: 4, of which 3 were waited for; matrix products, arithmetic and copies ran while one was open for 0% of the time, Pallas kernels for 9%

profile of v1, /device:TPU:1, one launch (start us, length us, event | category | flops | bytes accessed | tf_op | source)
XLA Modules:
  0.0 138.6 jit_solution(9380558275387808609)
XLA Ops:
  7.2 1.8 %pack.1 = bf16[144,1024]{1,0:T(8,128)(2,1)} custom-call(bf16[1,128,512]{2,1,0:T(8,128)(2,1)} %rk_ref.1, bf16[1,128,512]{2,1,0:T(8,128)(2,1)} %rv_ref.1, bf16[1,16,512]{2,1,0:T(8,128)(2,1)} %pk_ref.1, bf16[1,16,512]{2,1,0:T(8,128)(2,1)} %pv_ref.1), custom_call_target="tpu_custom_call" | custom-call | flops 1000 | bytes 600000 | tf_op jit(solution)/shard_map/pack/pallas_call | solution.py:423
  9.0 1.4 %shards.1 = bf16[64,16,128]{2,1,0:T(8,128)(2,1)} custom-call(f32[16,120]{1,0:T(8,128)} %adapter_ref.1), custom_call_target="tpu_custom_call" | custom-call | flops 1000 | bytes 300000 | tf_op jit(solution)/shard_map/shards/pallas_call | solution.py:444
  10.5 14.8 %all-to-all-start = ((bf16[64,16,128]{2,1,0:T(8,128)(2,1)}), bf16[64,16,128]{2,1,0:T(8,128)(2,1)S(1)}, u32[]{:S(2)}, u32[]{:S(2)}) async-start(bf16[64,16,128]{2,1,0:T(8,128)(2,1)} %shards.1), calls=%async_computation | async-start | bytes 524288 | tf_op jit(solution)/shard_map/all_to_all | solution.py:532
  26.0 11.3 %all-to-all-done.parts_ref = bf16[64,16,128]{2,1,0:T(8,128)(2,1)S(1)} async-done(((bf16[64,16,128]{2,1,0:T(8,128)(2,1)}), bf16[64,16,128]{2,1,0:T(8,128)(2,1)S(1)}, u32[]{:S(2)}, u32[]{:S(2)}) %all-to-all-start) | async-done | bytes 262176 | tf_op jit(solution)/shard_map/all_to_all | solution.py:532
  37.3 1.1 copy-done.1
  38.4 1.1 copy-done.2
  40.9 3.0 %prepare.1 = (bf16[128,5120]{1,0:T(8,128)(2,1)S(1)}, bf16[16,128]{1,0:T(8,128)(2,1)S(1)}, bf16[16,2560]{1,0:T(8,128)(2,1)S(1)}, bf16[2560,128]{1,0:T(8,128)(2,1)...) custom-call(s32[1]{0:T(128)} %bitcast.place_ref, ...), custom_call_target="tpu_custom_call" | custom-call | flops 80000000 | bytes 6000000 | tf_op jit(solution)/shard_map/prepare/pallas_call | solution.py:134
  43.9 1.1 copy-done.5
  45.0 0.9 copy-done.6
  45.9 0.9 copy-done.7
  46.8 0.9 copy-done.8
  47.6 0.8 copy-done.9
  50.2 6.5 %all-gather.2.cloned.1.call-done.kv_ref = bf16[1152,1024]{1,0:T(8,128)(2,1)} async-done(((bf16[144,1024]{1,0:T(8,128)(2,1)}), bf16[1152,1024]{1,0:T(8,128)(2,1)}) %all-gather.2.cloned.1.call-update) | async-done | bytes 2359312 | tf_op jit(solution)/shard_map/all_gather | solution.py:544
  56.8 8.3 %attend.1 = (bf16[128,2560]{1,0:T(8,128)(2,1)}, bf16[128,2560]{1,0:T(8,128)(2,1)}, bf16[1152,1024]{1,0:T(8,128)(2,1)}) custom-call(s32[18]{0:T(128)} %copy-done.12, f32[1280,128]{1,0:T(8,128)} %copy-done.9, bf16[2560,128]{1,0:T(8,128)(2,1)} %copy-done.6, bf16[2560,128]{1,0:T(8,128)(2,1)} %copy-done.7, bf16[128,2560]{1,0:T(8,128)(2,1)} %copy-done.8, ...), custom_call_target="tpu_custom_call" | custom-call | flops 3800000000 | bytes 8000000 | tf_op jit(solution)/shard_map/attend/pallas_call | solution.py:327
  65.1 3.3 %pieces.1 = bf16[64,16,128]{2,1,0:T(8,128)(2,1)} custom-call(bf16[128,2560]{1,0:T(8,128)(2,1)} %get-tuple-element.31.out_t_ref, bf16[16,128]{1,0:T(8,128)(2,1)} %copy-done.11, bf16[16,2560]{1,0:T(8,128)(2,1)} %copy-done.10, bf16[128,5120]{1,0:T(8,128)(2,1)} %copy-done.5), custom_call_target="tpu_custom_call" | custom-call | flops 199999995904 | bytes 2500000 | tf_op jit(solution)/shard_map/pieces/pallas_call | solution.py:384
  68.4 14.2 %all-to-all-start.1 = ((bf16[64,16,128]{2,1,0:T(8,128)(2,1)}), bf16[64,16,128]{2,1,0:T(8,128)(2,1)S(1)}, u32[]{:S(2)}, u32[]{:S(2)}) async-start(bf16[64,16,128]{2,1,0:T(8,128)(2,1)} %pieces.1), calls=%async_computation.1 | async-start | bytes 524288 | tf_op jit(solution)/shard_map/all_to_all | solution.py:532
  82.6 2.2 %turn.1 = bf16[128,2560]{1,0:T(8,128)(2,1)} custom-call(bf16[128,2560]{1,0:T(8,128)(2,1)} %get-tuple-element.35.turned_ref), custom_call_target="tpu_custom_call" | custom-call | flops 1000000 | bytes 1300000 | tf_op jit(solution)/shard_map/turn/pallas_call | solution.py:403
  84.8 9.8 %all-to-all-done.1.parts_ref = bf16[64,16,128]{2,1,0:T(8,128)(2,1)S(1)} async-done(((bf16[64,16,128]{2,1,0:T(8,128)(2,1)}), bf16[64,16,128]{2,1,0:T(8,128)(2,1)S(1)}, u32[]{:S(2)}, u32[]{:S(2)}) %all-to-all-start.1) | async-done | bytes 262176 | tf_op jit(solution)/shard_map/all_to_all | solution.py:532
  94.6 0.7 copy-done.13
  95.3 1.7 %group_sum.1 = f32[8,16,128]{2,1,0:T(8,128)} custom-call(bf16[64,16,128]{2,1,0:T(8,128)(2,1)} %copy-done.13), custom_call_target="tpu_custom_call" | custom-call | flops 200000 | bytes 400000 | tf_op jit(solution)/shard_map/group_sum/pallas_call | solution.py:462
  97.0 14.5 %all_to_all.20.parts_ref = f32[8,16,128]{2,1,0:T(8,128)} all-to-all(f32[8,16,128]{2,1,0:T(8,128)} %group_sum.1), channel_id=1, replica_groups=mesh['resp'=8,'fsdp'=64] {'resp'}, dimensions={0} | all-to-all | bytes 131072 | tf_op jit(solution)/shard_map/all_to_all | solution.py:532
  111.5 1.6 %norm.1 = (f32[16,128]{1,0:T(8,128)}, f32[64,1,128]{2,1,0:T(1,128)}) custom-call(f32[8,16,128]{2,1,0:T(8,128)} %all_to_all.20.parts_ref), custom_call_target="tpu_custom_call" | custom-call | flops 100000 | bytes 100000 | tf_op jit(solution)/shard_map/norm/pallas_call | solution.py:481
  113.1 16.9 %all_to_all.21.squares_ref = f32[64,1,128]{2,1,0:T(1,128)} all-to-all(f32[64,1,128]{2,1,0:T(1,128)} %get-tuple-element.40), channel_id=1, replica_groups=mesh['resp'=8,'fsdp'=64] {'fsdp'}, dimensions={0} | all-to-all | bytes 65536 | tf_op jit(solution)/shard_map/all_to_all | solution.py:532
  130.0 1.7 %finish.1 = (bf16[1,128,512]{2,1,0:T(8,128)(2,1)}, bf16[1,128,512]{2,1,0:T(8,128)(2,1)}, bf16[1,16,512]{2,1,0:T(8,128)(2,1)}, bf16[1,16,512]{2,1,0:T(8,128)(2,1)}, f32[16,120]{1,0:T(8,128)}) custom-call(bf16[144,1024]{1,0:T(8,128)(2,1)} %reduce-scatter.2.cloned.1.call-done.kv_ref, f32[16,128]{1,0:T(8,128)} %get-tuple-element.39.owned_ref, ...), custom_call_target="tpu_custom_call" | custom-call | flops 100000 | bytes 800000 | tf_op jit(solution)/shard_map/finish/pallas_call | solution.py:515
  (25 shorter events, 3.2 us)
Async XLA Ops:
  7.2 30.2 %copy-start = (bf16[1,128,5120]{2,1,0:T(8,128)(2,1)S(1)}, bf16[1,128,5120]{2,1,0:T(8,128)(2,1)}, u32[]{:S(2)}) copy-start(bf16[1,128,5120]{2,1,0:T(8,128)(2,1)} %param.19) | copy-start | bytes 3932164
  7.2 49.6 %all-gather.2.cloned.1.call-start = ((), (), s32[]{:S(2)}) async-start(), calls=%async_computation.5 | async-start | bytes 2654208 | tf_op jit(solution)/shard_map/all_gather | solution.py:544
  10.5 26.8 %all-to-all-start = ((bf16[64,16,128]{2,1,0:T(8,128)(2,1)}), bf16[64,16,128]{2,1,0:T(8,128)(2,1)S(1)}, u32[]{:S(2)}, u32[]{:S(2)}) async-start(bf16[64,16,128]{2,1,0:T(8,128)(2,1)} %shards.1), calls=%async_computation | async-start | bytes 524288 | tf_op jit(solution)/shard_map/all_to_all | solution.py:532
  25.3 104.7 %reduce-scatter.2.cloned.1.call-start = ((), (), s32[]{:S(2)}) async-start(), calls=%async_computation.6 | async-start | bytes 2654208 | tf_op jit(solution)/shard_map/reduce_scatter | solution.py:551
  37.3 1.1 copy-start.1
  38.4 1.1 copy-start.2
  39.5 0.7 copy-start.3
  40.2 0.7 copy-start.4
  43.9 1.1 copy-start.5
  45.0 0.9 copy-start.6
  45.9 0.9 copy-start.7
  46.8 0.9 copy-start.8
  47.6 0.8 copy-start.9
  48.5 0.6 copy-start.10
  49.1 0.6 copy-start.11
  49.7 0.5 copy-start.12
  68.4 26.2 %all-to-all-start.1 = ((bf16[64,16,128]{2,1,0:T(8,128)(2,1)}), bf16[64,16,128]{2,1,0:T(8,128)(2,1)S(1)}, u32[]{:S(2)}, u32[]{:S(2)}) async-start(bf16[64,16,128]{2,1,0:T(8,128)(2,1)} %pieces.1), calls=%async_computation.1 | async-start | bytes 524288 | tf_op jit(solution)/shard_map/all_to_all | solution.py:532
  94.6 0.7 copy-start.13
Sparse Core Ops, SparseCore 0:
  10.1 46.6 all-gather.1
  65.2 47.3 reduce-scatter.1

commit v2 on v1

--- a/solution.py
+++ b/solution.py
@@ -161,11 +161,11 @@
 
 
 def attend_kernel(
-    list_ref, bias_hbm, qs_hbm, gs_hbm, gt_hbm, kv_ref,
-    out_ref, turned_ref, kv_grad_ref,
-    bias_ref, qs_ref, gs_ref, gt_ref, keys_ref, score_ref, acc_ref, peak_ref, total_ref, inner_ref,
-    sums_ref, zero_ref,
-    in_sem, place_sem, prompt_in_sem, prompt_sem, block_sem,
+    list_ref, bias_hbm, qs_hbm, gs_hbm, gt_hbm, low_t_hbm, low_in_hbm, out_cot_hbm, kv_ref,
+    wide_out, turned_out, kv_grad_ref,
+    bias_ref, qs_ref, gs_ref, gt_ref, low_t_ref, low_in_ref, out_cot_ref, keys_ref, score_ref, acc_ref,
+    peak_ref, total_ref, inner_ref, wide_ref, turned_ref, sums_ref, zero_ref,
+    in_sem, q_sem, bias_sem, place_sem, prompt_in_sem, prompt_sem, block_sem, wide_sem, turned_sem,
 ):
     c = SCALE * LOG2E
     n_blocks = block_sem.shape[0]
@@ -180,9 +180,30 @@
     def load(src, dst, i):
         return pltpu.make_async_copy(src, dst, in_sem.at[i])
 
-    load_q, load_bias, load_g, load_gt = (
-        load(qs_hbm, qs_ref, 0), load(bias_hbm, bias_ref, 1), load(gs_hbm, gs_ref, 2), load(gt_hbm, gt_ref, 3)
-    )
+    later = [
+        load(src, dst, i)
+        for i, (src, dst) in enumerate(
+            (
+                (gt_hbm, gt_ref),
+                (low_t_hbm, low_t_ref),
+                (low_in_hbm, low_in_ref),
+                (out_cot_hbm, out_cot_ref),
+                (gs_hbm, gs_ref),
+            )
+        )
+    ]
+    load_q = [
+        pltpu.make_async_copy(
+            qs_hbm.at[pl.ds(h * group, group)], qs_ref.at[pl.ds(h * group, group)], q_sem.at[h]
+        )
+        for h in range(KV_HEADS)
+    ]
+
+    def load_bias(i):
+        return pltpu.make_async_copy(
+            bias_hbm.at[rows_of(i, width)], bias_ref.at[rows_of(i, width)], bias_sem.at[i]
+        )
+
     prompt_in = [
         pltpu.make_async_copy(
             kv_ref.at[pl.ds(i * (TOK + PRE), PRE)], keys_ref.at[pl.ds(i * PRE, PRE)], prompt_in_sem.at[i]
@@ -198,13 +219,19 @@
         bring(i).start()
         return carry
 
+    def start_bias(i, carry):
+        load_bias(i).start()
+        return carry
+
     for copy in prompt_in:
         copy.start()
-    load_q.start()
+    load_q[0].start()
+    lax.fori_loop(0, steps, start_bias, 0)
     lax.fori_loop(first, count, start, 0)
-    load_bias.start()
-    load_g.start()
-    load_gt.start()
+    for copy in load_q[1:]:
+        copy.start()
+    for copy in later:
+        copy.start()
 
     zero_ref[...] = jnp.zeros_like(zero_ref)
     peak_ref[...] = jnp.full_like(peak_ref, HIDDEN)
@@ -229,11 +256,10 @@
 
         return at + jnp.where(hit, 1, 0)
 
-    lax.fori_loop(0, n_blocks, unseen, first)
     for copy in prompt_in:
         copy.wait()
-    load_q.wait()
-    load_bias.wait()
+    for copy in load_q:
+        copy.wait()
 
     def cols(h):
         return slice(h * group, (h + 1) * group)
@@ -244,6 +270,7 @@
             return carry
 
         lax.fori_loop(jnp.maximum(i * JOIN, first), jnp.minimum((i + 1) * JOIN, count), arrive, 0)
+        load_bias(i).wait()
         rows = rows_of(i, width)
         bias = spread(bias_ref[rows, :])
         for h in range(KV_HEADS):
@@ -253,6 +280,7 @@
         return carry
 
     lax.fori_loop(0, steps, score_step, 0)
+    lax.fori_loop(0, n_blocks, unseen, first)
     peak = jnp.max(peak_ref[...], axis=0, keepdims=True) * c
     peak_ref[...] = jnp.broadcast_to(peak, peak_ref.shape)
 
@@ -269,15 +297,23 @@
     lax.fori_loop(0, steps, value_step, 0)
     inverse = 1.0 / jnp.sum(total_ref[...], axis=0, keepdims=True)
     total_ref[...] = jnp.broadcast_to(inverse, total_ref.shape)
-    load_g.wait()
-    load_gt.wait()
+    for copy in later:
+        copy.wait()
+    projected_t = jnp.zeros((RANK, TOK), jnp.float32)
     for i in range(Q_HEADS):
         part = slice(i * TOK, (i + 1) * TOK)
         rounded = (acc_ref[:, part] * inverse[:, part]).astype(jnp.bfloat16)
-        out_ref[:, part] = rounded
+        projected_t += dot(low_in_ref[:, part], rounded, NN)
+        wide_ref[:, part] = (adapter_scale * dot(low_t_ref[...], rounded, NT)).astype(jnp.bfloat16)
         across = gt_ref[:, part].astype(jnp.float32) * rounded.astype(jnp.float32)
         inner_ref[:, part] = jnp.broadcast_to(jnp.sum(across, axis=0, keepdims=True), (8, TOK))
     acc_ref[...] = jnp.zeros_like(acc_ref)
+    split = acc_ref.shape[1]
+    wide_ref[:, split:] = (
+        adapter_scale * dot(projected_t.astype(jnp.bfloat16), out_cot_ref[...], NN)
+    ).astype(jnp.bfloat16)
+    send_wide = pltpu.make_async_copy(wide_ref, wide_out, wide_sem.at[0])
+    send_wide.start()
 
     def back_step(i, carry):
         rows = rows_of(i, width)
@@ -307,8 +343,13 @@
     ]
     for copy in prompts:
         copy.start()
-    turned_ref[...] = (acc_ref[...] * SCALE).astype(jnp.bfloat16)
-    for copy in prompts:
+    back = []
+    for h in range(KV_HEADS):
+        part = pl.ds(h * group, group)
+        turned_ref[:, cols(h)] = (acc_ref[:, cols(h)] * SCALE).astype(jnp.bfloat16)
+        back.append(pltpu.make_async_copy(turned_ref.at[:, part], turned_out.at[:, part], turned_sem.at[h]))
+        back[-1].start()
+    for copy in prompts + back + [send_wide]:
         copy.wait()
 
     def finished(b2, carry):
@@ -318,78 +359,81 @@
     lax.fori_loop(0, n_blocks, finished, 0)
 
 
-def attend(blocks, bias, qs, gs, gt, kv, n_resp):
+def attend(blocks, bias, qs, gs, gt, low_t, low_in, out_cot, kv, n_resp):
     smem = pl.BlockSpec(memory_space=pltpu.SMEM)
-    vmem = pl.BlockSpec(memory_space=pltpu.VMEM)
     hbm = pl.BlockSpec(memory_space=pl.ANY)
     split = qs.shape[0]
+    wide = split + out_cot.shape[1]
     rows, columns = bias.shape[0], kv.shape[1]
     return pl.pallas_call(
         attend_kernel,
         out_shape=(
-            jax.ShapeDtypeStruct((HEAD, split), jnp.bfloat16),
+            jax.ShapeDtypeStruct((RANK, wide), jnp.bfloat16),
             jax.ShapeDtypeStruct((HEAD, split), jnp.bfloat16),
             jax.ShapeDtypeStruct(kv.shape, jnp.bfloat16),
         ),
-        in_specs=[smem] + [hbm] * 5,
-        out_specs=[vmem, vmem, hbm],
+        in_specs=[smem] + [hbm] * 8,
+        out_specs=[hbm] * 3,
         scratch_shapes=[
             pltpu.VMEM(bias.shape, jnp.float32),
             pltpu.VMEM(qs.shape, jnp.bfloat16),
             pltpu.VMEM(gs.shape, jnp.bfloat16),
             pltpu.VMEM(gt.shape, jnp.bfloat16),
+            pltpu.VMEM(low_t.shape, jnp.bfloat16),
+            pltpu.VMEM(low_in.shape, jnp.bfloat16),
+            pltpu.VMEM(out_cot.shape, jnp.bfloat16),
             pltpu.VMEM((rows, columns), jnp.bfloat16),
             pltpu.VMEM((rows, split), jnp.float32),
             pltpu.VMEM((HEAD, split), jnp.float32),
             pltpu.VMEM((8, split), jnp.float32),
             pltpu.VMEM((8, split), jnp.float32),
             pltpu.VMEM((8, split), jnp.float32),
+            pltpu.VMEM((RANK, wide), jnp.bfloat16),
+            pltpu.VMEM((HEAD, split), jnp.bfloat16),
             pltpu.VMEM((rows, columns), jnp.bfloat16),
             pltpu.VMEM((BLK, columns), jnp.bfloat16),
-            pltpu.SemaphoreType.DMA((4,)),
+            pltpu.SemaphoreType.DMA((5,)),
+            pltpu.SemaphoreType.DMA((KV_HEADS,)),
+            pltpu.SemaphoreType.DMA((rows // (JOIN * BLK),)),
             pltpu.SemaphoreType.DMA((rows // BLK,)),
             pltpu.SemaphoreType.DMA((n_resp,)),
             pltpu.SemaphoreType.DMA((n_resp,)),
             pltpu.SemaphoreType.DMA((n_resp * (TOK // BLK),)),
+            pltpu.SemaphoreType.DMA((1,)),
+            pltpu.SemaphoreType.DMA((KV_HEADS,)),
         ],
         compiler_params=pltpu.CompilerParams(vmem_limit_bytes=56 * 1024 * 1024),
         cost_estimate=pl.CostEstimate(
             flops=3_800_000_000, bytes_accessed=8_000_000, transcendentals=3_000_000
         ),
         name="attend",
-    )(blocks, bias, qs, gs, gt, kv)
-
-
-def pieces_kernel(out_t_ref, low_t_ref, low_in_ref, out_cot_ref, parts_ref, wide_ref):
-    projected_t = jnp.zeros((RANK, TOK), jnp.float32)
-    for i in range(Q_HEADS):
-        part = slice(i * TOK, (i + 1) * TOK)
-        projected_t += dot(low_in_ref[:, part], out_t_ref[:, part], NN)
-        wide_ref[:, part] = adapter_scale * dot(low_t_ref[...], out_t_ref[:, part], NT)
-    split = out_t_ref.shape[1]
-    wide_ref[:, split:] = adapter_scale * dot(projected_t.astype(jnp.bfloat16), out_cot_ref[...], NN)
-    parts_ref[...] = jnp.zeros_like(parts_ref)
+    )(blocks, bias, qs, gs, gt, low_t, low_in, out_cot, kv)
+
+
+def pieces_kernel(wide_ref, parts_ref, whole_ref):
+    whole_ref[...] = wide_ref[...].astype(jnp.float32)
     n_parts = parts_ref.shape[0]
-    piece = wide_ref.shape[1] // n_parts
+    piece = whole_ref.shape[1] // n_parts
+    fill = jnp.zeros((RANK, LANES - piece), jnp.float32)
     for i in range(n_parts):
-        parts_ref[i, :, :piece] = wide_ref[:, i * piece : (i + 1) * piece].astype(jnp.bfloat16)
+        part = whole_ref[:, i * piece : (i + 1) * piece]
+        parts_ref[i] = jnp.concatenate([part, fill], axis=1).astype(jnp.bfloat16)
 
 
 PIECES_FLOPS = 200_000_000_000
 
 
-def pieces(out_t, low_t, low_in, out_cot, n_fsdp):
+def pieces(wide, n_fsdp):
     vmem = pl.BlockSpec(memory_space=pltpu.VMEM)
-    wide = out_t.shape[1] + out_cot.shape[1]
     return pl.pallas_call(
         pieces_kernel,
         out_shape=jax.ShapeDtypeStruct((n_fsdp, RANK, LANES), jnp.bfloat16),
-        in_specs=[vmem] * 4,
+        in_specs=[vmem],
         out_specs=vmem,
-        scratch_shapes=[pltpu.VMEM((RANK, wide), jnp.float32)],
-        cost_estimate=pl.CostEstimate(flops=PIECES_FLOPS, bytes_accessed=2_500_000, transcendentals=0),
+        scratch_shapes=[pltpu.VMEM(wide.shape, jnp.float32)],
+        cost_estimate=pl.CostEstimate(flops=PIECES_FLOPS, bytes_accessed=500_000, transcendentals=0),
         name="pieces",
-    )(out_t, low_t, low_in, out_cot)
+    )(wide)
 
 
 def turn_kernel(turned_ref, out_ref):
@@ -451,81 +495,37 @@
     )(adapter)
 
 
-def group_sum_kernel(parts_ref, copies_ref):
-    total = jnp.sum(parts_ref[...].astype(jnp.float32), axis=0)
-    for i in range(copies_ref.shape[0]):
-        copies_ref[i] = total
-
-
-def group_sum(parts, copies):
-    vmem = pl.BlockSpec(memory_space=pltpu.VMEM)
-    return pl.pallas_call(
-        group_sum_kernel,
-        out_shape=jax.ShapeDtypeStruct((copies,) + parts.shape[1:], jnp.float32),
-        in_specs=[vmem],
-        out_specs=vmem,
-        cost_estimate=pl.CostEstimate(flops=200_000, bytes_accessed=400_000, transcendentals=0),
-        name="group_sum",
-    )(parts)
-
-
-def norm_kernel(parts_ref, owned_ref, squares_ref):
-    owned = jnp.sum(parts_ref[...], axis=0)
-    owned_ref[...] = owned
-    squares = jnp.sum(jnp.sum(owned * owned, axis=0, keepdims=True), axis=1, keepdims=True)
-    squares_ref[...] = jnp.broadcast_to(squares[None], squares_ref.shape)
-
-
-def norm(parts, copies):
-    vmem = pl.BlockSpec(memory_space=pltpu.VMEM)
-    return pl.pallas_call(
-        norm_kernel,
-        out_shape=(
-            jax.ShapeDtypeStruct(parts.shape[1:], jnp.float32),
-            jax.ShapeDtypeStruct((copies, 1, LANES), jnp.float32),
-        ),
-        in_specs=[vmem],
-        out_specs=[vmem] * 2,
-        cost_estimate=pl.CostEstimate(flops=100_000, bytes_accessed=100_000, transcendentals=0),
-        name="norm",
-    )(parts)
-
-
-def finish_kernel(
-    kv_ref, owned_ref, squares_ref, first_ref, second_ref,
-    rk_ref, rv_ref, pk_ref, pv_ref, update_ref,
-):
+def unpack_kernel(kv_ref, rk_ref, rv_ref, pk_ref, pv_ref):
     half = rk_ref.shape[2]
     rk_ref[0] = kv_ref[PRE:, :half]
     rv_ref[0] = kv_ref[PRE:, half:]
     pk_ref[0] = kv_ref[:PRE, :half]
     pv_ref[0] = kv_ref[:PRE, half:]
-    width = first_ref.shape[1]
-    squares = jnp.sum(squares_ref[...], axis=0)[:, :width]
-    clip_factor = max_norm / jnp.maximum(jnp.sqrt(squares), max_norm)
-    scaled = owned_ref[:, :width] * clip_factor
-    moment = beta_first * first_ref[...] + (1.0 - beta_first) * scaled
-    second_new = beta_second * second_ref[...] + (1.0 - beta_second) * scaled * scaled
-    update_ref[...] = moment / first_fix / (jnp.sqrt(second_new / second_fix) + adam_eps)
-
-
-def finish(kv_sum, owned, squares, first, second):
+
+
+def unpack(kv_sum):
     vmem = pl.BlockSpec(memory_space=pltpu.VMEM)
     half = kv_sum.shape[1] // 2
     return pl.pallas_call(
-        finish_kernel,
+        unpack_kernel,
         out_shape=(
             jax.ShapeDtypeStruct((1, TOK, half), jnp.bfloat16),
             jax.ShapeDtypeStruct((1, TOK, half), jnp.bfloat16),
             jax.ShapeDtypeStruct((1, PRE, half), jnp.bfloat16),
             jax.ShapeDtypeStruct((1, PRE, half), jnp.bfloat16),
-            jax.ShapeDtypeStruct(first.shape, jnp.float32),
         ),
-        in_specs=[vmem] * 5,
-        out_specs=[vmem] * 5,
-        cost_estimate=pl.CostEstimate(flops=100_000, bytes_accessed=800_000, transcendentals=4_000),
-        name="finish",
-    )(kv_sum, owned, squares, first, second)
+        in_specs=[vmem],
+        out_specs=[vmem] * 4,
+        cost_estimate=pl.CostEstimate(flops=1_000, bytes_accessed=600_000, transcendentals=0),
+        name="unpack",
+    )(kv_sum)
+
+
+def adam_update_of(gradient, first_state, second_state, clip_factor):
+    scaled = gradient * clip_factor
+    moment = beta_first * first_state + (1.0 - beta_first) * scaled
+    second_new = beta_second * second_state + (1.0 - beta_second) * scaled * scaled
+    return moment / first_fix / (jnp.sqrt(second_new / second_fix) + adam_eps)
 
 
 def swap(x, axis):
@@ -547,18 +547,20 @@
         place, lengths, tree_mask[0], advantages, gathered, queries[0], output_grad[0],
         attention_output_gradient[0],
     )
-    out_t, turned, kv_grad = attend(blocks, bias, qs, gs, gt, kv, n_resp)
+    wide, turned, kv_grad = attend(blocks, bias, qs, gs, gt, low_t, low_in, out_cot, kv, n_resp)
     kv_sum = lax.psum_scatter(kv_grad, "resp", scatter_dimension=0, tiled=True)
-    arrived = swap(pieces(out_t, low_t, low_in, out_cot, n_fsdp), "fsdp")
+    arrived = swap(pieces(wide, n_fsdp), "fsdp")
     q_grad = turn(turned)
     arrived, q_grad = lax.optimization_barrier((arrived, q_grad))
-    copies = group_sum(arrived, n_resp)
-    owned, squares = norm(swap(copies, "resp"), n_fsdp)
+    group = jnp.sum(arrived.astype(jnp.float32), axis=0)
+    owned = jnp.sum(swap(jnp.broadcast_to(group, (n_resp,) + group.shape), "resp"), axis=0)
+    squares = jnp.broadcast_to(jnp.sum(owned * owned), (n_fsdp, 1, LANES))
     squares = swap(squares, "fsdp")
-    key_sum, value_sum, prompt_key_sum, prompt_value_sum, update = finish(
-        kv_sum, owned, squares, first_moment, second_moment
-    )
-    return (q_grad[None], key_sum, value_sum, prompt_key_sum, prompt_value_sum, update)
+    sums = unpack(kv_sum)
+    squares, sums = lax.optimization_barrier((squares, sums))
+    clip_factor = max_norm / jnp.maximum(jnp.sqrt(jnp.sum(squares[:, 0, 0])), max_norm)
+    update = adam_update_of(owned[:, : adapter.shape[1]], first_moment, second_moment, clip_factor)
+    return (q_grad[None],) + tuple(sums) + (update,)
 
 
 def solution(mesh):

time: 139 us -> 136 us (0.978)
  blocking collectives: 31.5 us -> 14.4 us
  waiting for transfers between devices: 27.7 us -> 35.5 us
  starting transfers between devices: 29.1 us -> 36.6 us
  Pallas kernels: 25 us -> 20.3 us
  other arithmetic: 0 us -> 1.97 us
    all_to_all x2 -> x1, blocking collectives: 31.5 us -> 14.4 us  [swap(): return lax.all_to_all(x, axis, 0, 0, tiled=True)]
    all_to_all x2 -> x3, waiting for transfers between devices: 21.1 us -> 28.7 us  [swap(): return lax.all_to_all(x, axis, 0, 0, tiled=True)]
    all_to_all x2 -> x3, starting transfers between devices: 29 us -> 36.5 us  [swap(): return lax.all_to_all(x, axis, 0, 0, tiled=True)]
    pallas_call x4 -> x2, Pallas kernels: 13.3 us -> 10 us  [the longest x1 8.34 us: attend(): pl.pallas_call(attend_kernel, out_shape=(jax.ShapeDtypeStruct((RANK, wide...]
    pallas_call x1, Pallas kernels: 3.27 us -> 1.86 us  [pieces(): pl.pallas_call(pieces_kernel, out_shape=jax.ShapeDtypeStruct((n_fsdp, RAN...]
    unnamed x28 -> x30, local copies, waits for them, and re-layouts: 10.5 us -> 9.8 us
  transfers between devices with their start and end apart: 4 -> 5, of which waited for: 3 -> 4; matrix products, arithmetic and copies ran while one was open for 0% -> 1% of each run, Pallas kernels for 9% -> 8%
where the time goes in v2:
time: 136 us; the launch traced here: 135 us
  starting transfers between devices  36.6 us (27%)
  waiting for transfers between devices  35.5 us (26%)
  Pallas kernels  20.3 us (15%)
  between operations  15.5 us (11%)
  blocking collectives  14.4 us (11%)
  local copies, waits for them, and re-layouts  11.1 us (8%)
  other arithmetic  1.97 us (1%)
    all_to_all x3, starting transfers between devices, swap(): return lax.all_to_all(x, axis, 0, 0, tiled=True)  36.5 us
    all_to_all x3, waiting for transfers between devices, swap(): return lax.all_to_all(x, axis, 0, 0, tiled=True)  28.7 us
    all_to_all x1, blocking collectives, swap(): return lax.all_to_all(x, axis, 0, 0, tiled=True)  14.4 us
    unnamed x30, local copies, waits for them, and re-layouts  9.8 us
    pallas_call x1, Pallas kernels, attend(): pl.pallas_call(attend_kernel, out_shape=(jax.ShapeDtypeStruct((RANK, wide...  8.34 us
    all_gather x1, waiting for transfers between devices, on_device(): kv = lax.all_gather(own_kv, 'resp', axis=0, tiled=True)  6.67 us
    pallas_call x1, Pallas kernels, prepare(): pl.pallas_call(prepare_kernel, out_shape=(jax.ShapeDtypeStruct(og.shape,...  3.04 us
  transfers between devices with their start and end apart: 5, of which 4 were waited for; matrix products, arithmetic and copies ran while one was open for 1% of the time, Pallas kernels for 8%

profile of v2, /device:TPU:1, one launch (start us, length us, event | category | flops | bytes accessed | tf_op | source)
XLA Modules:
  0.0 135.4 jit_solution(5520469177696657555)
XLA Ops:
  7.2 1.8 %pack.1 = bf16[144,1024]{1,0:T(8,128)(2,1)} custom-call(bf16[1,128,512]{2,1,0:T(8,128)(2,1)} %rk_ref.1, bf16[1,128,512]{2,1,0:T(8,128)(2,1)} %rv_ref.1, bf16[1,16,512]{2,1,0:T(8,128)(2,1)} %pk_ref.1, bf16[1,16,512]{2,1,0:T(8,128)(2,1)} %pv_ref.1), custom_call_target="tpu_custom_call" | custom-call | flops 1000 | bytes 600000 | tf_op jit(solution)/shard_map/pack/pallas_call | solution.py:467
  9.1 1.4 %shards.1 = bf16[64,16,128]{2,1,0:T(8,128)(2,1)} custom-call(f32[16,120]{1,0:T(8,128)} %adapter_ref.1), custom_call_target="tpu_custom_call" | custom-call | flops 1000 | bytes 300000 | tf_op jit(solution)/shard_map/shards/pallas_call | solution.py:488
  10.5 14.8 %all-to-all-start = ((bf16[64,16,128]{2,1,0:T(8,128)(2,1)}), bf16[64,16,128]{2,1,0:T(8,128)(2,1)S(1)}, u32[]{:S(2)}, u32[]{:S(2)}) async-start(bf16[64,16,128]{2,1,0:T(8,128)(2,1)} %shards.1), calls=%async_computation | async-start | bytes 524288 | tf_op jit(solution)/shard_map/all_to_all | solution.py:532
  26.0 11.3 %all-to-all-done.parts_ref = bf16[64,16,128]{2,1,0:T(8,128)(2,1)S(1)} async-done(((bf16[64,16,128]{2,1,0:T(8,128)(2,1)}), bf16[64,16,128]{2,1,0:T(8,128)(2,1)S(1)}, u32[]{:S(2)}, u32[]{:S(2)}) %all-to-all-start) | async-done | bytes 262176 | tf_op jit(solution)/shard_map/all_to_all | solution.py:532
  37.4 1.1 copy-done.1
  38.4 1.1 copy-done.2
  39.5 0.7 copy-done.3
  40.9 3.0 %prepare.1 = (bf16[128,5120]{1,0:T(8,128)(2,1)S(1)}, bf16[16,128]{1,0:T(8,128)(2,1)S(1)}, bf16[16,2560]{1,0:T(8,128)(2,1)S(1)}, bf16[2560,128]{1,0:T(8,128)(2,1)...) custom-call(s32[1]{0:T(128)} %bitcast.place_ref, ...), custom_call_target="tpu_custom_call" | custom-call | flops 80000000 | bytes 6000000 | tf_op jit(solution)/shard_map/prepare/pallas_call | solution.py:134
  43.9 1.1 copy-done.5
  45.0 0.8 copy-done.6
  45.9 0.8 copy-done.7
  46.7 0.9 copy-done.8
  47.6 0.8 copy-done.9
  50.2 6.7 %all-gather.2.cloned.1.call-done.kv_ref = bf16[1152,1024]{1,0:T(8,128)(2,1)} async-done(((bf16[144,1024]{1,0:T(8,128)(2,1)}), bf16[1152,1024]{1,0:T(8,128)(2,1)}) %all-gather.2.cloned.1.call-update) | async-done | bytes 2359312 | tf_op jit(solution)/shard_map/all_gather | solution.py:544
  56.9 8.3 %attend.1 = (bf16[16,7680]{1,0:T(8,128)(2,1)}, bf16[128,2560]{1,0:T(8,128)(2,1)}, bf16[1152,1024]{1,0:T(8,128)(2,1)}) custom-call(s32[18]{0:T(128)} %copy-done.12, f32[1280,128]{1,0:T(8,128)} %copy-done.9, bf16[2560,128]{1,0:T(8,128)(2,1)} %copy-done.6, bf16[2560,128]{1,0:T(8,128)(2,1)} %copy-done.7, bf16[128,2560]{1,0:T(8,128)(2,1)} %copy-done.8, ...), custom_call_target="tpu_custom_call" | custom-call | flops 3800000000 | bytes 8000000 | tf_op jit(solution)/shard_map/attend/pallas_call | solution.py:368
  65.2 1.9 %pieces.1 = bf16[64,16,128]{2,1,0:T(8,128)(2,1)} custom-call(bf16[16,7680]{1,0:T(8,128)(2,1)} %get-tuple-element.36.wide_ref), custom_call_target="tpu_custom_call" | custom-call | flops 199999995904 | bytes 500000 | tf_op jit(solution)/shard_map/pieces/pallas_call | solution.py:428
  67.1 14.2 %all-to-all-start.1 = ((bf16[64,16,128]{2,1,0:T(8,128)(2,1)}), bf16[64,16,128]{2,1,0:T(8,128)(2,1)S(1)}, u32[]{:S(2)}, u32[]{:S(2)}) async-start(bf16[64,16,128]{2,1,0:T(8,128)(2,1)} %pieces.1), calls=%async_computation.1 | async-start | bytes 524288 | tf_op jit(solution)/shard_map/all_to_all | solution.py:532
  81.3 2.2 %turn.1 = bf16[128,2560]{1,0:T(8,128)(2,1)} custom-call(bf16[128,2560]{1,0:T(8,128)(2,1)} %get-tuple-element.37.turned_ref), custom_call_target="tpu_custom_call" | custom-call | flops 1000000 | bytes 1300000 | tf_op jit(solution)/shard_map/turn/pallas_call | solution.py:447
  83.5 9.8 %all-to-all-done.1 = bf16[64,16,128]{2,1,0:T(8,128)(2,1)S(1)} async-done(((bf16[64,16,128]{2,1,0:T(8,128)(2,1)}), bf16[64,16,128]{2,1,0:T(8,128)(2,1)S(1)}, u32[]{:S(2)}, u32[]{:S(2)}) %all-to-all-start.1) | async-done | bytes 262176 | tf_op jit(solution)/shard_map/all_to_all | solution.py:532
  93.4 14.4 %all_to_all.20 = f32[8,16,128]{2,1,0:T(8,128)S(1)} all-to-all(f32[8,16,128]{2,1,0:T(8,128)S(1)} %broadcast_in_dim.10), channel_id=1, replica_groups=mesh['resp'=8,'fsdp'=64] {'resp'}, dimensions={0} | all-to-all | bytes 131072 | tf_op jit(solution)/shard_map/all_to_all | solution.py:532
  108.5 1.3 broadcast_in_dim.11
  109.7 7.5 %all-to-all-start.3 = ((f32[64,1,128]{2,1,0:T(1,128)}), f32[64,1,128]{2,1,0:T(1,128)S(1)}, u32[]{:S(2)}, u32[]{:S(2)}) async-start(f32[64,1,128]{2,1,0:T(1,128)} %broadcast_in_dim.11), calls=%async_computation.3 | async-start | bytes 65536 | tf_op jit(solution)/shard_map/all_to_all | solution.py:532
  117.3 1.7 %unpack.1 = (bf16[1,128,512]{2,1,0:T(8,128)(2,1)}, bf16[1,128,512]{2,1,0:T(8,128)(2,1)}, bf16[1,16,512]{2,1,0:T(8,128)(2,1)}, bf16[1,16,512]{2,1,0:T(8,128)(2,1)}) custom-call(bf16[144,1024]{1,0:T(8,128)(2,1)} %reduce-scatter.2.cloned.1.call-done.kv_ref), custom_call_target="tpu_custom_call" | custom-call | flops 1000 | bytes 600000 | tf_op jit(solution)/shard_map/unpack/pallas_call | solution.py:509
  118.9 7.6 %all-to-all-done.3 = f32[64,1,128]{2,1,0:T(1,128)S(1)} async-done(((f32[64,1,128]{2,1,0:T(1,128)}), f32[64,1,128]{2,1,0:T(1,128)S(1)}, u32[]{:S(2)}, u32[]{:S(2)}) %all-to-all-start.3) | async-done | bytes 32800 | tf_op jit(solution)/shard_map/all_to_all | solution.py:532
  (33 shorter events, 4.5 us)
Async XLA Ops:
  7.2 30.2 %copy-start = (bf16[1,128,5120]{2,1,0:T(8,128)(2,1)S(1)}, bf16[1,128,5120]{2,1,0:T(8,128)(2,1)}, u32[]{:S(2)}) copy-start(bf16[1,128,5120]{2,1,0:T(8,128)(2,1)} %param.19) | copy-start | bytes 3932164
  7.2 49.7 %all-gather.2.cloned.1.call-start = ((), (), s32[]{:S(2)}) async-start(), calls=%async_computation.5 | async-start | bytes 2654208 | tf_op jit(solution)/shard_map/all_gather | solution.py:544
  10.5 26.8 %all-to-all-start = ((bf16[64,16,128]{2,1,0:T(8,128)(2,1)}), bf16[64,16,128]{2,1,0:T(8,128)(2,1)S(1)}, u32[]{:S(2)}, u32[]{:S(2)}) async-start(bf16[64,16,128]{2,1,0:T(8,128)(2,1)} %shards.1), calls=%async_computation | async-start | bytes 524288 | tf_op jit(solution)/shard_map/all_to_all | solution.py:532
  25.3 91.9 %reduce-scatter.2.cloned.1.call-start = ((), (), s32[]{:S(2)}) async-start(), calls=%async_computation.6 | async-start | bytes 2654208 | tf_op jit(solution)/shard_map/reduce_scatter | solution.py:551
  37.3 1.1 copy-start.1
  38.4 1.1 copy-start.2
  39.5 0.7 copy-start.3
  40.2 0.7 copy-start.4
  43.9 1.1 copy-start.5
  45.0 0.9 copy-start.6
  45.9 0.8 copy-start.7
  46.7 0.9 copy-start.8
  47.6 0.8 copy-start.9
  48.5 0.6 copy-start.10
  49.1 0.6 copy-start.11
  49.7 0.5 copy-start.12
  67.1 60.8 %copy-start.13 = (f32[16,120]{1,0:T(8,128)S(1)}, f32[16,120]{1,0:T(8,128)}, u32[]{:S(2)}) copy-start(f32[16,120]{1,0:T(8,128)} %param.25) | copy-start | bytes 23044
  67.1 60.8 %copy-start.14 = (f32[16,120]{1,0:T(8,128)S(1)}, f32[16,120]{1,0:T(8,128)}, u32[]{:S(2)}) copy-start(f32[16,120]{1,0:T(8,128)} %param.24) | copy-start | bytes 23044
  67.1 26.2 %all-to-all-start.1 = ((bf16[64,16,128]{2,1,0:T(8,128)(2,1)}), bf16[64,16,128]{2,1,0:T(8,128)(2,1)S(1)}, u32[]{:S(2)}, u32[]{:S(2)}) async-start(bf16[64,16,128]{2,1,0:T(8,128)(2,1)} %pieces.1), calls=%async_computation.1 | async-start | bytes 524288 | tf_op jit(solution)/shard_map/all_to_all | solution.py:532
  109.7 16.8 %all-to-all-start.3 = ((f32[64,1,128]{2,1,0:T(1,128)}), f32[64,1,128]{2,1,0:T(1,128)S(1)}, u32[]{:S(2)}, u32[]{:S(2)}) async-start(f32[64,1,128]{2,1,0:T(1,128)} %broadcast_in_dim.11), calls=%async_computation.3 | async-start | bytes 65536 | tf_op jit(solution)/shard_map/all_to_all | solution.py:532
Sparse Core Ops, SparseCore 0:
  10.1 46.7 all-gather.1
  65.4 47.3 reduce-scatter.1

commit v3 on v2

--- a/solution.py
+++ b/solution.py
@@ -162,9 +162,9 @@
 
 def attend_kernel(
     list_ref, bias_hbm, qs_hbm, gs_hbm, gt_hbm, low_t_hbm, low_in_hbm, out_cot_hbm, kv_ref,
-    wide_out, turned_out, kv_grad_ref,
+    parts_out, turned_out, kv_grad_ref,
     bias_ref, qs_ref, gs_ref, gt_ref, low_t_ref, low_in_ref, out_cot_ref, keys_ref, score_ref, acc_ref,
-    peak_ref, total_ref, inner_ref, wide_ref, turned_ref, sums_ref, zero_ref,
+    peak_ref, total_ref, inner_ref, wide_ref, parts_ref, turned_ref, sums_ref, zero_ref,
     in_sem, q_sem, bias_sem, place_sem, prompt_in_sem, prompt_sem, block_sem, wide_sem, turned_sem,
 ):
     c = SCALE * LOG2E
@@ -225,11 +225,10 @@
 
     for copy in prompt_in:
         copy.start()
-    load_q[0].start()
+    for copy in load_q:
+        copy.start()
     lax.fori_loop(0, steps, start_bias, 0)
     lax.fori_loop(first, count, start, 0)
-    for copy in load_q[1:]:
-        copy.start()
     for copy in later:
         copy.start()
 
@@ -280,7 +279,6 @@
         return carry
 
     lax.fori_loop(0, steps, score_step, 0)
-    lax.fori_loop(0, n_blocks, unseen, first)
     peak = jnp.max(peak_ref[...], axis=0, keepdims=True) * c
     peak_ref[...] = jnp.broadcast_to(peak, peak_ref.shape)
 
@@ -295,6 +293,7 @@
         return carry
 
     lax.fori_loop(0, steps, value_step, 0)
+    lax.fori_loop(0, n_blocks, unseen, first)
     inverse = 1.0 / jnp.sum(total_ref[...], axis=0, keepdims=True)
     total_ref[...] = jnp.broadcast_to(inverse, total_ref.shape)
     for copy in later:
@@ -304,16 +303,20 @@
         part = slice(i * TOK, (i + 1) * TOK)
         rounded = (acc_ref[:, part] * inverse[:, part]).astype(jnp.bfloat16)
         projected_t += dot(low_in_ref[:, part], rounded, NN)
-        wide_ref[:, part] = (adapter_scale * dot(low_t_ref[...], rounded, NT)).astype(jnp.bfloat16)
+        wide_ref[:, part] = adapter_scale * dot(low_t_ref[...], rounded, NT)
         across = gt_ref[:, part].astype(jnp.float32) * rounded.astype(jnp.float32)
         inner_ref[:, part] = jnp.broadcast_to(jnp.sum(across, axis=0, keepdims=True), (8, TOK))
     acc_ref[...] = jnp.zeros_like(acc_ref)
     split = acc_ref.shape[1]
-    wide_ref[:, split:] = (
-        adapter_scale * dot(projected_t.astype(jnp.bfloat16), out_cot_ref[...], NN)
-    ).astype(jnp.bfloat16)
-    send_wide = pltpu.make_async_copy(wide_ref, wide_out, wide_sem.at[0])
-    send_wide.start()
+    wide_ref[:, split:] = adapter_scale * dot(projected_t.astype(jnp.bfloat16), out_cot_ref[...], NN)
+    n_parts = parts_ref.shape[0]
+    piece = wide_ref.shape[1] // n_parts
+    fill = jnp.zeros((RANK, LANES - piece), jnp.float32)
+    for i in range(n_parts):
+        part = wide_ref[:, i * piece : (i + 1) * piece]
+        parts_ref[i] = jnp.concatenate([part, fill], axis=1).astype(jnp.bfloat16)
+    send_parts = pltpu.make_async_copy(parts_ref, parts_out, wide_sem.at[0])
+    send_parts.start()
 
     def back_step(i, carry):
         rows = rows_of(i, width)
@@ -349,7 +352,7 @@
         turned_ref[:, cols(h)] = (acc_ref[:, cols(h)] * SCALE).astype(jnp.bfloat16)
         back.append(pltpu.make_async_copy(turned_ref.at[:, part], turned_out.at[:, part], turned_sem.at[h]))
         back[-1].start()
-    for copy in prompts + back + [send_wide]:
+    for copy in prompts + back + [send_parts]:
         copy.wait()
 
     def finished(b2, carry):
@@ -359,7 +362,7 @@
     lax.fori_loop(0, n_blocks, finished, 0)
 
 
-def attend(blocks, bias, qs, gs, gt, low_t, low_in, out_cot, kv, n_resp):
+def attend(blocks, bias, qs, gs, gt, low_t, low_in, out_cot, kv, n_fsdp, n_resp):
     smem = pl.BlockSpec(memory_space=pltpu.SMEM)
     hbm = pl.BlockSpec(memory_space=pl.ANY)
     split = qs.shape[0]
@@ -368,7 +371,7 @@
     return pl.pallas_call(
         attend_kernel,
         out_shape=(
-            jax.ShapeDtypeStruct((RANK, wide), jnp.bfloat16),
+            jax.ShapeDtypeStruct((n_fsdp, RANK, LANES), jnp.bfloat16),
             jax.ShapeDtypeStruct((HEAD, split), jnp.bfloat16),
             jax.ShapeDtypeStruct(kv.shape, jnp.bfloat16),
         ),
@@ -388,7 +391,8 @@
             pltpu.VMEM((8, split), jnp.float32),
             pltpu.VMEM((8, split), jnp.float32),
             pltpu.VMEM((8, split), jnp.float32),
-            pltpu.VMEM((RANK, wide), jnp.bfloat16),
+            pltpu.VMEM((RANK, wide), jnp.float32),
+            pltpu.VMEM((n_fsdp, RANK, LANES), jnp.bfloat16),
             pltpu.VMEM((HEAD, split), jnp.bfloat16),
             pltpu.VMEM((rows, columns), jnp.bfloat16),
             pltpu.VMEM((BLK, columns), jnp.bfloat16),
@@ -410,30 +414,24 @@
     )(blocks, bias, qs, gs, gt, low_t, low_in, out_cot, kv)
 
 
-def pieces_kernel(wide_ref, parts_ref, whole_ref):
-    whole_ref[...] = wide_ref[...].astype(jnp.float32)
-    n_parts = parts_ref.shape[0]
-    piece = whole_ref.shape[1] // n_parts
-    fill = jnp.zeros((RANK, LANES - piece), jnp.float32)
-    for i in range(n_parts):
-        part = whole_ref[:, i * piece : (i + 1) * piece]
-        parts_ref[i] = jnp.concatenate([part, fill], axis=1).astype(jnp.bfloat16)
-
-
-PIECES_FLOPS = 200_000_000_000
-
-
-def pieces(wide, n_fsdp):
-    vmem = pl.BlockSpec(memory_space=pltpu.VMEM)
-    return pl.pallas_call(
-        pieces_kernel,
-        out_shape=jax.ShapeDtypeStruct((n_fsdp, RANK, LANES), jnp.bfloat16),
-        in_specs=[vmem],
-        out_specs=vmem,
-        scratch_shapes=[pltpu.VMEM(wide.shape, jnp.float32)],
-        cost_estimate=pl.CostEstimate(flops=PIECES_FLOPS, bytes_accessed=500_000, transcendentals=0),
-        name="pieces",
-    )(wide)
+def hold_kernel(parts_ref, same_ref):
+    del parts_ref, same_ref
+
+
+HOLD_FLOPS = 200_000_000_000
+
+
+def hold(parts):
+    hbm = pl.BlockSpec(memory_space=pl.ANY)
+    return pl.pallas_call(
+        hold_kernel,
+        out_shape=jax.ShapeDtypeStruct(parts.shape, parts.dtype),
+        in_specs=[hbm],
+        out_specs=hbm,
+        input_output_aliases={0: 0},
+        cost_estimate=pl.CostEstimate(flops=HOLD_FLOPS, bytes_accessed=500_000, transcendentals=0),
+        name="hold",
+    )(parts)
 
 
 def turn_kernel(turned_ref, out_ref):
@@ -521,10 +519,10 @@
     )(kv_sum)
 
 
-def adam_update_of(gradient, first_state, second_state, clip_factor):
+def adam_update_of(gradient, first_term, second_term, clip_factor):
     scaled = gradient * clip_factor
-    moment = beta_first * first_state + (1.0 - beta_first) * scaled
-    second_new = beta_second * second_state + (1.0 - beta_second) * scaled * scaled
+    moment = first_term + (1.0 - beta_first) * scaled
+    second_new = second_term + (1.0 - beta_second) * scaled * scaled
     return moment / first_fix / (jnp.sqrt(second_new / second_fix) + adam_eps)
 
 
@@ -547,19 +545,24 @@
         place, lengths, tree_mask[0], advantages, gathered, queries[0], output_grad[0],
         attention_output_gradient[0],
     )
-    wide, turned, kv_grad = attend(blocks, bias, qs, gs, gt, low_t, low_in, out_cot, kv, n_resp)
+    parts, turned, kv_grad = attend(
+        blocks, bias, qs, gs, gt, low_t, low_in, out_cot, kv, n_fsdp, n_resp
+    )
     kv_sum = lax.psum_scatter(kv_grad, "resp", scatter_dimension=0, tiled=True)
-    arrived = swap(pieces(wide, n_fsdp), "fsdp")
+    arrived = swap(hold(parts), "fsdp")
     q_grad = turn(turned)
     arrived, q_grad = lax.optimization_barrier((arrived, q_grad))
     group = jnp.sum(arrived.astype(jnp.float32), axis=0)
     owned = jnp.sum(swap(jnp.broadcast_to(group, (n_resp,) + group.shape), "resp"), axis=0)
+    owned, first_term, second_term = lax.optimization_barrier(
+        (owned, beta_first * first_moment, beta_second * second_moment)
+    )
     squares = jnp.broadcast_to(jnp.sum(owned * owned), (n_fsdp, 1, LANES))
     squares = swap(squares, "fsdp")
     sums = unpack(kv_sum)
     squares, sums = lax.optimization_barrier((squares, sums))
     clip_factor = max_norm / jnp.maximum(jnp.sqrt(jnp.sum(squares[:, 0, 0])), max_norm)
-    update = adam_update_of(owned[:, : adapter.shape[1]], first_moment, second_moment, clip_factor)
+    update = adam_update_of(owned[:, : adapter.shape[1]], first_term, second_term, clip_factor)
     return (q_grad[None],) + tuple(sums) + (update,)
 
 

time: 136 us -> 136 us (level)
  blocking collectives: 14.4 us -> 0 us
  starting transfers between devices: 36.6 us -> 45.1 us
  waiting for transfers between devices: 35.5 us -> 42.8 us
  Pallas kernels: 20.3 us -> 17.9 us
    all_to_all x1 -> x0, blocking collectives: 14.4 us -> none  [swap(): return lax.all_to_all(x, axis, 0, 0, tiled=True)]
    all_to_all x3 -> x4, starting transfers between devices: 36.5 us -> 45 us  [swap(): return lax.all_to_all(x, axis, 0, 0, tiled=True)]
    all_to_all x3 -> x4, waiting for transfers between devices: 28.7 us -> 36 us  [swap(): return lax.all_to_all(x, axis, 0, 0, tiled=True)]
    pallas_call x2, Pallas kernels: 10.2 us -> 7.81 us  [the longest x1 7.8 us: attend(): pl.pallas_call(attend_kernel, out_shape=(jax.ShapeDtypeStruct((n_fsdp, RA...]
  transfers between devices with their start and end apart: 5 -> 6, of which waited for: 4 -> 5; matrix products, arithmetic and copies ran while one was open for 1% -> 2% of each run, Pallas kernels for 8% -> 6%
where the time goes in v3:
time: 136 us; the launch traced here: 135 us
  starting transfers between devices  45.1 us (33%)
  waiting for transfers between devices  42.8 us (31%)
  Pallas kernels  17.9 us (13%)
  between operations  15.6 us (11%)
  local copies, waits for them, and re-layouts  11.7 us (9%)
  other arithmetic  1.97 us (1%)
    all_to_all x4, starting transfers between devices, swap(): return lax.all_to_all(x, axis, 0, 0, tiled=True)  45 us
    all_to_all x4, waiting for transfers between devices, swap(): return lax.all_to_all(x, axis, 0, 0, tiled=True)  36 us
    unnamed x30, local copies, waits for them, and re-layouts  9.77 us
    pallas_call x1, Pallas kernels, attend(): pl.pallas_call(attend_kernel, out_shape=(jax.ShapeDtypeStruct((n_fsdp, RA...  7.8 us
    all_gather x1, waiting for transfers between devices, on_device(): kv = lax.all_gather(own_kv, 'resp', axis=0, tiled=True)  6.67 us
    pallas_call x1, Pallas kernels, prepare(): pl.pallas_call(prepare_kernel, out_shape=(jax.ShapeDtypeStruct(og.shape,...  3.04 us
  transfers between devices with their start and end apart: 6, of which 5 were waited for; matrix products, arithmetic and copies ran while one was open for 2% of the time, Pallas kernels for 6%

profile of v3, /device:TPU:1, one launch (start us, length us, event | category | flops | bytes accessed | tf_op | source)
XLA Modules:
  0.0 135.0 jit_solution(6220935617828151046)
XLA Ops:
  7.2 1.8 %pack.1 = bf16[144,1024]{1,0:T(8,128)(2,1)} custom-call(bf16[1,128,512]{2,1,0:T(8,128)(2,1)} %rk_ref.1, bf16[1,128,512]{2,1,0:T(8,128)(2,1)} %rv_ref.1, bf16[1,16,512]{2,1,0:T(8,128)(2,1)} %pk_ref.1, bf16[1,16,512]{2,1,0:T(8,128)(2,1)} %pv_ref.1), custom_call_target="tpu_custom_call" | custom-call | flops 1000 | bytes 600000 | tf_op jit(solution)/shard_map/pack/pallas_call | solution.py:465
  9.0 1.4 %shards.1 = bf16[64,16,128]{2,1,0:T(8,128)(2,1)} custom-call(f32[16,120]{1,0:T(8,128)} %adapter_ref.1), custom_call_target="tpu_custom_call" | custom-call | flops 1000 | bytes 300000 | tf_op jit(solution)/shard_map/shards/pallas_call | solution.py:486
  10.5 14.8 %all-to-all-start = ((bf16[64,16,128]{2,1,0:T(8,128)(2,1)}), bf16[64,16,128]{2,1,0:T(8,128)(2,1)S(1)}, u32[]{:S(2)}, u32[]{:S(2)}) async-start(bf16[64,16,128]{2,1,0:T(8,128)(2,1)} %shards.1), calls=%async_computation | async-start | bytes 524288 | tf_op jit(solution)/shard_map/all_to_all | solution.py:530
  26.0 11.3 %all-to-all-done.parts_ref = bf16[64,16,128]{2,1,0:T(8,128)(2,1)S(1)} async-done(((bf16[64,16,128]{2,1,0:T(8,128)(2,1)}), bf16[64,16,128]{2,1,0:T(8,128)(2,1)S(1)}, u32[]{:S(2)}, u32[]{:S(2)}) %all-to-all-start) | async-done | bytes 262176 | tf_op jit(solution)/shard_map/all_to_all | solution.py:530
  37.3 1.1 copy-done.1
  38.4 1.1 copy-done.2
  39.5 0.7 copy-done.3
  40.9 3.0 %prepare.1 = (bf16[128,5120]{1,0:T(8,128)(2,1)S(1)}, bf16[16,128]{1,0:T(8,128)(2,1)S(1)}, bf16[16,2560]{1,0:T(8,128)(2,1)S(1)}, bf16[2560,128]{1,0:T(8,128)(2,1)...) custom-call(s32[1]{0:T(128)} %bitcast.place_ref, ...), custom_call_target="tpu_custom_call" | custom-call | flops 80000000 | bytes 6000000 | tf_op jit(solution)/shard_map/prepare/pallas_call | solution.py:134
  43.9 1.1 copy-done.5
  45.0 0.8 copy-done.6
  45.8 0.9 copy-done.7
  46.7 0.9 copy-done.8
  47.6 0.8 copy-done.9
  50.2 6.7 %all-gather.2.cloned.1.call-done.kv_ref = bf16[1152,1024]{1,0:T(8,128)(2,1)} async-done(((bf16[144,1024]{1,0:T(8,128)(2,1)}), bf16[1152,1024]{1,0:T(8,128)(2,1)}) %all-gather.2.cloned.1.call-update) | async-done | bytes 2359312 | tf_op jit(solution)/shard_map/all_gather | solution.py:542
  56.8 7.8 %attend.1 = (bf16[64,16,128]{2,1,0:T(8,128)(2,1)}, bf16[128,2560]{1,0:T(8,128)(2,1)}, bf16[1152,1024]{1,0:T(8,128)(2,1)}) custom-call(s32[18]{0:T(128)} %copy-done.12, f32[1280,128]{1,0:T(8,128)} %copy-done.9, bf16[2560,128]{1,0:T(8,128)(2,1)} %copy-done.6, bf16[2560,128]{1,0:T(8,128)(2,1)} %copy-done.7, bf16[128,2560]{1,0:T(8,128)(2,1)} %copy-done.8, ...), custom_call_target="tpu_custom_call" | custom-call | flops 3800000000 | bytes 8000000 | tf_op jit(solution)/shard_map/attend/pallas_call | solution.py:371
  64.7 14.1 %all-to-all-start.1 = ((bf16[64,16,128]{2,1,0:T(8,128)(2,1)}), bf16[64,16,128]{2,1,0:T(8,128)(2,1)S(1)}, u32[]{:S(2)}, u32[]{:S(2)}) async-start(bf16[64,16,128]{2,1,0:T(8,128)(2,1)} %hold.1), calls=%async_computation.1 | async-start | bytes 524288 | tf_op jit(solution)/shard_map/all_to_all | solution.py:530
  78.8 2.2 %turn.1 = bf16[128,2560]{1,0:T(8,128)(2,1)} custom-call(bf16[128,2560]{1,0:T(8,128)(2,1)} %get-tuple-element.40.turned_ref), custom_call_target="tpu_custom_call" | custom-call | flops 1000000 | bytes 1300000 | tf_op jit(solution)/shard_map/turn/pallas_call | solution.py:445
  80.9 9.8 %all-to-all-done.1 = bf16[64,16,128]{2,1,0:T(8,128)(2,1)S(1)} async-done(((bf16[64,16,128]{2,1,0:T(8,128)(2,1)}), bf16[64,16,128]{2,1,0:T(8,128)(2,1)S(1)}, u32[]{:S(2)}, u32[]{:S(2)}) %all-to-all-start.1) | async-done | bytes 262176 | tf_op jit(solution)/shard_map/all_to_all | solution.py:530
  91.5 7.9 %all-to-all-start.2 = ((f32[8,16,128]{2,1,0:T(8,128)}), f32[8,16,128]{2,1,0:T(8,128)S(1)}, u32[]{:S(2)}, u32[]{:S(2)}) async-start(f32[8,16,128]{2,1,0:T(8,128)} %broadcast_in_dim.10), calls=%async_computation.2 | async-start | bytes 131072 | tf_op jit(solution)/shard_map/all_to_all | solution.py:530
  99.4 7.3 %all-to-all-done.2 = f32[8,16,128]{2,1,0:T(8,128)S(1)} async-done(((f32[8,16,128]{2,1,0:T(8,128)}), f32[8,16,128]{2,1,0:T(8,128)S(1)}, u32[]{:S(2)}, u32[]{:S(2)}) %all-to-all-start.2) | async-done | bytes 65568 | tf_op jit(solution)/shard_map/all_to_all | solution.py:530
  107.3 1.3 broadcast_in_dim.11
  108.6 8.2 %all-to-all-start.3 = ((f32[64,1,128]{2,1,0:T(1,128)}), f32[64,1,128]{2,1,0:T(1,128)S(1)}, u32[]{:S(2)}, u32[]{:S(2)}) async-start(f32[64,1,128]{2,1,0:T(1,128)} %broadcast_in_dim.11), calls=%async_computation.3 | async-start | bytes 65536 | tf_op jit(solution)/shard_map/all_to_all | solution.py:530
  116.8 1.7 %unpack.1 = (bf16[1,128,512]{2,1,0:T(8,128)(2,1)}, bf16[1,128,512]{2,1,0:T(8,128)(2,1)}, bf16[1,16,512]{2,1,0:T(8,128)(2,1)}, bf16[1,16,512]{2,1,0:T(8,128)(2,1)}) custom-call(bf16[144,1024]{1,0:T(8,128)(2,1)} %reduce-scatter.2.cloned.1.call-done.kv_ref), custom_call_target="tpu_custom_call" | custom-call | flops 1000 | bytes 600000 | tf_op jit(solution)/shard_map/unpack/pallas_call | solution.py:507
  118.5 7.6 %all-to-all-done.3 = f32[64,1,128]{2,1,0:T(1,128)S(1)} async-done(((f32[64,1,128]{2,1,0:T(1,128)}), f32[64,1,128]{2,1,0:T(1,128)S(1)}, u32[]{:S(2)}, u32[]{:S(2)}) %all-to-all-start.3) | async-done | bytes 32800 | tf_op jit(solution)/shard_map/all_to_all | solution.py:530
  (35 shorter events, 5.2 us)
Async XLA Ops:
  7.2 30.2 %copy-start = (bf16[1,128,5120]{2,1,0:T(8,128)(2,1)S(1)}, bf16[1,128,5120]{2,1,0:T(8,128)(2,1)}, u32[]{:S(2)}) copy-start(bf16[1,128,5120]{2,1,0:T(8,128)(2,1)} %param.19) | copy-start | bytes 3932164
  7.2 49.7 %all-gather.2.cloned.1.call-start = ((), (), s32[]{:S(2)}) async-start(), calls=%async_computation.5 | async-start | bytes 2654208 | tf_op jit(solution)/shard_map/all_gather | solution.py:542
  10.5 26.8 %all-to-all-start = ((bf16[64,16,128]{2,1,0:T(8,128)(2,1)}), bf16[64,16,128]{2,1,0:T(8,128)(2,1)S(1)}, u32[]{:S(2)}, u32[]{:S(2)}) async-start(bf16[64,16,128]{2,1,0:T(8,128)(2,1)} %shards.1), calls=%async_computation | async-start | bytes 524288 | tf_op jit(solution)/shard_map/all_to_all | solution.py:530
  25.3 91.5 %reduce-scatter.2.cloned.1.call-start = ((), (), s32[]{:S(2)}) async-start(), calls=%async_computation.6 | async-start | bytes 2654208 | tf_op jit(solution)/shard_map/reduce_scatter | solution.py:551
  37.3 1.1 copy-start.1
  38.4 1.1 copy-start.2
  39.5 0.7 copy-start.3
  40.2 0.7 copy-start.4
  43.9 1.1 copy-start.5
  45.0 0.8 copy-start.6
  45.8 0.9 copy-start.7
  46.7 0.9 copy-start.8
  47.6 0.8 copy-start.9
  48.4 0.6 copy-start.10
  49.1 0.6 copy-start.11
  49.6 0.5 copy-start.12
  64.7 34.7 %copy-start.13 = (f32[16,120]{1,0:T(8,128)S(1)}, f32[16,120]{1,0:T(8,128)}, u32[]{:S(2)}) copy-start(f32[16,120]{1,0:T(8,128)} %param.25) | copy-start | bytes 23044
  64.7 34.7 %copy-start.14 = (f32[16,120]{1,0:T(8,128)S(1)}, f32[16,120]{1,0:T(8,128)}, u32[]{:S(2)}) copy-start(f32[16,120]{1,0:T(8,128)} %param.24) | copy-start | bytes 23044
  64.7 26.1 %all-to-all-start.1 = ((bf16[64,16,128]{2,1,0:T(8,128)(2,1)}), bf16[64,16,128]{2,1,0:T(8,128)(2,1)S(1)}, u32[]{:S(2)}, u32[]{:S(2)}) async-start(bf16[64,16,128]{2,1,0:T(8,128)(2,1)} %hold.1), calls=%async_computation.1 | async-start | bytes 524288 | tf_op jit(solution)/shard_map/all_to_all | solution.py:530
  91.5 15.2 %all-to-all-start.2 = ((f32[8,16,128]{2,1,0:T(8,128)}), f32[8,16,128]{2,1,0:T(8,128)S(1)}, u32[]{:S(2)}, u32[]{:S(2)}) async-start(f32[8,16,128]{2,1,0:T(8,128)} %broadcast_in_dim.10), calls=%async_computation.2 | async-start | bytes 131072 | tf_op jit(solution)/shard_map/all_to_all | solution.py:530
  108.6 17.5 %all-to-all-start.3 = ((f32[64,1,128]{2,1,0:T(1,128)}), f32[64,1,128]{2,1,0:T(1,128)S(1)}, u32[]{:S(2)}, u32[]{:S(2)}) async-start(f32[64,1,128]{2,1,0:T(1,128)} %broadcast_in_dim.11), calls=%async_computation.3 | async-start | bytes 65536 | tf_op jit(solution)/shard_map/all_to_all | solution.py:530
Sparse Core Ops, SparseCore 0:
  10.1 46.6 all-gather.1
  64.8 48.4 reduce-scatter.1

commit v4 on v3

--- a/solution.py
+++ b/solution.py
@@ -223,12 +223,11 @@
         load_bias(i).start()
         return carry
 
-    for copy in prompt_in:
+    load_bias(0).start()
+    for copy in load_q + prompt_in:
         copy.start()
-    for copy in load_q:
-        copy.start()
-    lax.fori_loop(0, steps, start_bias, 0)
     lax.fori_loop(first, count, start, 0)
+    lax.fori_loop(1, steps, start_bias, 0)
     for copy in later:
         copy.start()
 
@@ -519,6 +518,28 @@
     )(kv_sum)
 
 
+def norm_kernel(parts_ref, owned_ref, squares_ref):
+    owned = jnp.sum(parts_ref[...], axis=0)
+    owned_ref[...] = owned
+    squares = jnp.sum(jnp.sum(owned * owned, axis=0, keepdims=True), axis=1, keepdims=True)
+    squares_ref[...] = jnp.broadcast_to(squares[None], squares_ref.shape)
+
+
+def norm(parts, copies):
+    vmem = pl.BlockSpec(memory_space=pltpu.VMEM)
+    return pl.pallas_call(
+        norm_kernel,
+        out_shape=(
+            jax.ShapeDtypeStruct(parts.shape[1:], jnp.float32),
+            jax.ShapeDtypeStruct((copies, 1, LANES), jnp.float32),
+        ),
+        in_specs=[vmem],
+        out_specs=[vmem] * 2,
+        cost_estimate=pl.CostEstimate(flops=100_000, bytes_accessed=100_000, transcendentals=0),
+        name="norm",
+    )(parts)
+
+
 def adam_update_of(gradient, first_term, second_term, clip_factor):
     scaled = gradient * clip_factor
     moment = first_term + (1.0 - beta_first) * scaled
@@ -553,15 +574,15 @@
     q_grad = turn(turned)
     arrived, q_grad = lax.optimization_barrier((arrived, q_grad))
     group = jnp.sum(arrived.astype(jnp.float32), axis=0)
-    owned = jnp.sum(swap(jnp.broadcast_to(group, (n_resp,) + group.shape), "resp"), axis=0)
+    owned, squares = norm(swap(jnp.broadcast_to(group, (n_resp,) + group.shape), "resp"), n_fsdp)
     owned, first_term, second_term = lax.optimization_barrier(
         (owned, beta_first * first_moment, beta_second * second_moment)
     )
-    squares = jnp.broadcast_to(jnp.sum(owned * owned), (n_fsdp, 1, LANES))
     squares = swap(squares, "fsdp")
     sums = unpack(kv_sum)
     squares, sums = lax.optimization_barrier((squares, sums))
-    clip_factor = max_norm / jnp.maximum(jnp.sqrt(jnp.sum(squares[:, 0, 0])), max_norm)
+    total = jnp.sum(squares, axis=0)[:, : adapter.shape[1]]
+    clip_factor = max_norm / jnp.maximum(jnp.sqrt(total), max_norm)
     update = adam_update_of(owned[:, : adapter.shape[1]], first_term, second_term, clip_factor)
     return (q_grad[None],) + tuple(sums) + (update,)
 

time: 136 us -> 133 us (0.978)
  blocking collectives: 0 us -> 14.4 us
  starting transfers between devices: 45.1 us -> 37.3 us
  waiting for transfers between devices: 42.8 us -> 35.3 us
  local copies, waits for them, and re-layouts: 11.7 us -> 9.8 us
  Pallas kernels: 17.9 us -> 19.3 us
    all_to_all x0 -> x1, blocking collectives: none -> 14.4 us  [swap(): return lax.all_to_all(x, axis, 0, 0, tiled=True)]
    all_to_all x4 -> x3, starting transfers between devices: 45 us -> 37.2 us  [swap(): return lax.all_to_all(x, axis, 0, 0, tiled=True)]
    all_to_all x4 -> x3, waiting for transfers between devices: 36 us -> 28.7 us  [swap(): return lax.all_to_all(x, axis, 0, 0, tiled=True)]
    pallas_call x0 -> x1, Pallas kernels: none -> 1.55 us  [norm(): pl.pallas_call(norm_kernel, out_shape=(jax.ShapeDtypeStruct(parts.shape[1...]
  transfers between devices with their start and end apart: 6 -> 5, of which waited for: 5 -> 4; matrix products, arithmetic and copies ran while one was open for 2% -> 0% of each run, Pallas kernels for 6% -> 7%
where the time goes in v4:
time: 133 us; the launch traced here: 132 us
  starting transfers between devices  37.3 us (28%)
  waiting for transfers between devices  35.3 us (27%)
  Pallas kernels  19.3 us (15%)
  between operations  14.8 us (11%)
  blocking collectives  14.4 us (11%)
  local copies, waits for them, and re-layouts  9.8 us (7%)
  other arithmetic  1.5 us (1%)
    all_to_all x3, starting transfers between devices, swap(): return lax.all_to_all(x, axis, 0, 0, tiled=True)  37.2 us
    all_to_all x3, waiting for transfers between devices, swap(): return lax.all_to_all(x, axis, 0, 0, tiled=True)  28.7 us
    all_to_all x1, blocking collectives, swap(): return lax.all_to_all(x, axis, 0, 0, tiled=True)  14.4 us
    unnamed x30, local copies, waits for them, and re-layouts  9.79 us
    pallas_call x1, Pallas kernels, attend(): pl.pallas_call(attend_kernel, out_shape=(jax.ShapeDtypeStruct((n_fsdp, RA...  7.7 us
    all_gather x1, waiting for transfers between devices, on_device(): kv = lax.all_gather(own_kv, 'resp', axis=0, tiled=True)  6.6 us
    pallas_call x1, Pallas kernels, prepare(): pl.pallas_call(prepare_kernel, out_shape=(jax.ShapeDtypeStruct(og.shape,...  3.03 us
  transfers between devices with their start and end apart: 5, of which 4 were waited for; matrix products, arithmetic and copies ran while one was open for 0% of the time, Pallas kernels for 7%

profile of v4, /device:TPU:1, one launch (start us, length us, event | category | flops | bytes accessed | tf_op | source)
XLA Modules:
  0.0 132.5 jit_solution(13454057122386478094)
XLA Ops:
  7.2 1.8 %pack.1 = bf16[144,1024]{1,0:T(8,128)(2,1)} custom-call(bf16[1,128,512]{2,1,0:T(8,128)(2,1)} %rk_ref.1, bf16[1,128,512]{2,1,0:T(8,128)(2,1)} %rv_ref.1, bf16[1,16,512]{2,1,0:T(8,128)(2,1)} %pk_ref.1, bf16[1,16,512]{2,1,0:T(8,128)(2,1)} %pv_ref.1), custom_call_target="tpu_custom_call" | custom-call | flops 1000 | bytes 600000 | tf_op jit(solution)/shard_map/pack/pallas_call | solution.py:464
  9.0 1.4 %shards.1 = bf16[64,16,128]{2,1,0:T(8,128)(2,1)} custom-call(f32[16,120]{1,0:T(8,128)} %adapter_ref.1), custom_call_target="tpu_custom_call" | custom-call | flops 1000 | bytes 300000 | tf_op jit(solution)/shard_map/shards/pallas_call | solution.py:485
  10.5 14.8 %all-to-all-start = ((bf16[64,16,128]{2,1,0:T(8,128)(2,1)}), bf16[64,16,128]{2,1,0:T(8,128)(2,1)S(1)}, u32[]{:S(2)}, u32[]{:S(2)}) async-start(bf16[64,16,128]{2,1,0:T(8,128)(2,1)} %shards.1), calls=%async_computation | async-start | bytes 524288 | tf_op jit(solution)/shard_map/all_to_all | solution.py:551
  26.0 11.3 %all-to-all-done.parts_ref = bf16[64,16,128]{2,1,0:T(8,128)(2,1)S(1)} async-done(((bf16[64,16,128]{2,1,0:T(8,128)(2,1)}), bf16[64,16,128]{2,1,0:T(8,128)(2,1)S(1)}, u32[]{:S(2)}, u32[]{:S(2)}) %all-to-all-start) | async-done | bytes 262176 | tf_op jit(solution)/shard_map/all_to_all | solution.py:551
  37.3 1.1 copy-done.1
  38.4 1.1 copy-done.2
  39.5 0.7 copy-done.3
  40.9 3.0 %prepare.1 = (bf16[128,5120]{1,0:T(8,128)(2,1)S(1)}, bf16[16,128]{1,0:T(8,128)(2,1)S(1)}, bf16[16,2560]{1,0:T(8,128)(2,1)S(1)}, bf16[2560,128]{1,0:T(8,128)(2,1)...) custom-call(s32[1]{0:T(128)} %bitcast.place_ref, ...), custom_call_target="tpu_custom_call" | custom-call | flops 80000000 | bytes 6000000 | tf_op jit(solution)/shard_map/prepare/pallas_call | solution.py:134
  43.9 1.1 copy-done.5
  45.0 0.8 copy-done.6
  45.8 0.8 copy-done.7
  46.7 0.9 copy-done.8
  47.6 0.8 copy-done.9
  50.2 6.6 %all-gather.2.cloned.1.call-done.kv_ref = bf16[1152,1024]{1,0:T(8,128)(2,1)} async-done(((bf16[144,1024]{1,0:T(8,128)(2,1)}), bf16[1152,1024]{1,0:T(8,128)(2,1)}) %all-gather.2.cloned.1.call-update) | async-done | bytes 2359312 | tf_op jit(solution)/shard_map/all_gather | solution.py:563
  56.8 7.7 %attend.1 = (bf16[64,16,128]{2,1,0:T(8,128)(2,1)}, bf16[128,2560]{1,0:T(8,128)(2,1)}, bf16[1152,1024]{1,0:T(8,128)(2,1)}) custom-call(s32[18]{0:T(128)} %copy-done.12, f32[1280,128]{1,0:T(8,128)} %copy-done.9, bf16[2560,128]{1,0:T(8,128)(2,1)} %copy-done.6, bf16[2560,128]{1,0:T(8,128)(2,1)} %copy-done.7, bf16[128,2560]{1,0:T(8,128)(2,1)} %copy-done.8, ...), custom_call_target="tpu_custom_call" | custom-call | flops 3800000000 | bytes 8000000 | tf_op jit(solution)/shard_map/attend/pallas_call | solution.py:370
  64.5 14.3 %all-to-all-start.1 = ((bf16[64,16,128]{2,1,0:T(8,128)(2,1)}), bf16[64,16,128]{2,1,0:T(8,128)(2,1)S(1)}, u32[]{:S(2)}, u32[]{:S(2)}) async-start(bf16[64,16,128]{2,1,0:T(8,128)(2,1)} %hold.1), calls=%async_computation.1 | async-start | bytes 524288 | tf_op jit(solution)/shard_map/all_to_all | solution.py:551
  78.8 2.2 %turn.1 = bf16[128,2560]{1,0:T(8,128)(2,1)} custom-call(bf16[128,2560]{1,0:T(8,128)(2,1)} %get-tuple-element.42.turned_ref), custom_call_target="tpu_custom_call" | custom-call | flops 1000000 | bytes 1300000 | tf_op jit(solution)/shard_map/turn/pallas_call | solution.py:444
  81.0 9.8 %all-to-all-done.1 = bf16[64,16,128]{2,1,0:T(8,128)(2,1)S(1)} async-done(((bf16[64,16,128]{2,1,0:T(8,128)(2,1)}), bf16[64,16,128]{2,1,0:T(8,128)(2,1)S(1)}, u32[]{:S(2)}, u32[]{:S(2)}) %all-to-all-start.1) | async-done | bytes 262176 | tf_op jit(solution)/shard_map/all_to_all | solution.py:551
  90.9 14.4 %all_to_all.20.parts_ref = f32[8,16,128]{2,1,0:T(8,128)} all-to-all(f32[8,16,128]{2,1,0:T(8,128)S(1)} %broadcast_in_dim.7), channel_id=1, replica_groups=mesh['resp'=8,'fsdp'=64] {'resp'}, dimensions={0} | all-to-all | bytes 131072 | tf_op jit(solution)/shard_map/all_to_all | solution.py:551
  105.3 1.5 %norm.1 = (f32[16,128]{1,0:T(8,128)}, f32[64,1,128]{2,1,0:T(1,128)}) custom-call(f32[8,16,128]{2,1,0:T(8,128)} %all_to_all.20.parts_ref), custom_call_target="tpu_custom_call" | custom-call | flops 100000 | bytes 100000 | tf_op jit(solution)/shard_map/norm/pallas_call | solution.py:530
  106.8 8.1 %all-to-all-start.3 = ((f32[64,1,128]{2,1,0:T(1,128)}), f32[64,1,128]{2,1,0:T(1,128)S(1)}, u32[]{:S(2)}, u32[]{:S(2)}) async-start(f32[64,1,128]{2,1,0:T(1,128)} %get-tuple-element.45), calls=%async_computation.3 | async-start | bytes 65536 | tf_op jit(solution)/shard_map/all_to_all | solution.py:551
  115.0 1.7 %unpack.1 = (bf16[1,128,512]{2,1,0:T(8,128)(2,1)}, bf16[1,128,512]{2,1,0:T(8,128)(2,1)}, bf16[1,16,512]{2,1,0:T(8,128)(2,1)}, bf16[1,16,512]{2,1,0:T(8,128)(2,1)}) custom-call(bf16[144,1024]{1,0:T(8,128)(2,1)} %reduce-scatter.2.cloned.1.call-done.kv_ref), custom_call_target="tpu_custom_call" | custom-call | flops 1000 | bytes 600000 | tf_op jit(solution)/shard_map/unpack/pallas_call | solution.py:506
  116.7 7.5 %all-to-all-done.3 = f32[64,1,128]{2,1,0:T(1,128)S(1)} async-done(((f32[64,1,128]{2,1,0:T(1,128)}), f32[64,1,128]{2,1,0:T(1,128)S(1)}, u32[]{:S(2)}, u32[]{:S(2)}) %all-to-all-start.3) | async-done | bytes 32800 | tf_op jit(solution)/shard_map/all_to_all | solution.py:551
  124.3 1.3 %fusion.4 = f32[16,120]{1,0:T(8,128)} fusion(f32[16,120]{1,0:T(8,128)S(1)} %get-tuple-element.59, f32[16,120]{1,0:T(8,128)S(1)} %get-tuple-element.56, f32[16,128]{1,0:T(8,128)} %get-tuple-element.57, f32[120]{0:T(128)S(1)} %divide_bitcast_fusion), kind=kLoop, calls=%fused_computation.6 | loop fusion | flops 19200 | bytes 31200 | tf_op jit(solution)/shard_map/div | solution.py:547
  (33 shorter events, 2.7 us)
Async XLA Ops:
  7.2 30.2 %copy-start = (bf16[1,128,5120]{2,1,0:T(8,128)(2,1)S(1)}, bf16[1,128,5120]{2,1,0:T(8,128)(2,1)}, u32[]{:S(2)}) copy-start(bf16[1,128,5120]{2,1,0:T(8,128)(2,1)} %param.19) | copy-start | bytes 3932164
  7.2 49.6 %all-gather.2.cloned.1.call-start = ((), (), s32[]{:S(2)}) async-start(), calls=%async_computation.5 | async-start | bytes 2654208 | tf_op jit(solution)/shard_map/all_gather | solution.py:563
  10.5 26.8 %all-to-all-start = ((bf16[64,16,128]{2,1,0:T(8,128)(2,1)}), bf16[64,16,128]{2,1,0:T(8,128)(2,1)S(1)}, u32[]{:S(2)}, u32[]{:S(2)}) async-start(bf16[64,16,128]{2,1,0:T(8,128)(2,1)} %shards.1), calls=%async_computation | async-start | bytes 524288 | tf_op jit(solution)/shard_map/all_to_all | solution.py:551
  25.3 89.6 %reduce-scatter.2.cloned.1.call-start = ((), (), s32[]{:S(2)}) async-start(), calls=%async_computation.6 | async-start | bytes 2654208 | tf_op jit(solution)/shard_map/reduce_scatter | solution.py:572
  37.3 1.1 copy-start.1
  38.4 1.1 copy-start.2
  39.5 0.7 copy-start.3
  40.2 0.7 copy-start.4
  43.9 1.1 copy-start.5
  45.0 0.8 copy-start.6
  45.8 0.8 copy-start.7
  46.7 0.9 copy-start.8
  47.6 0.8 copy-start.9
  48.4 0.6 copy-start.10
  49.1 0.6 copy-start.11
  49.7 0.5 copy-start.12
  64.5 50.4 %copy-start.13 = (f32[16,120]{1,0:T(8,128)S(1)}, f32[16,120]{1,0:T(8,128)}, u32[]{:S(2)}) copy-start(f32[16,120]{1,0:T(8,128)} %param.25) | copy-start | bytes 23044
  64.5 50.4 %copy-start.14 = (f32[16,120]{1,0:T(8,128)S(1)}, f32[16,120]{1,0:T(8,128)}, u32[]{:S(2)}) copy-start(f32[16,120]{1,0:T(8,128)} %param.24) | copy-start | bytes 23044
  64.5 26.3 %all-to-all-start.1 = ((bf16[64,16,128]{2,1,0:T(8,128)(2,1)}), bf16[64,16,128]{2,1,0:T(8,128)(2,1)S(1)}, u32[]{:S(2)}, u32[]{:S(2)}) async-start(bf16[64,16,128]{2,1,0:T(8,128)(2,1)} %hold.1), calls=%async_computation.1 | async-start | bytes 524288 | tf_op jit(solution)/shard_map/all_to_all | solution.py:551
  106.8 17.4 %all-to-all-start.3 = ((f32[64,1,128]{2,1,0:T(1,128)}), f32[64,1,128]{2,1,0:T(1,128)S(1)}, u32[]{:S(2)}, u32[]{:S(2)}) async-start(f32[64,1,128]{2,1,0:T(1,128)} %get-tuple-element.45), calls=%async_computation.3 | async-start | bytes 65536 | tf_op jit(solution)/shard_map/all_to_all | solution.py:551
Sparse Core Ops, SparseCore 0:
  10.1 46.6 all-gather.1
  64.6 47.4 reduce-scatter.1

commit v5 on v4

--- a/solution.py
+++ b/solution.py
@@ -519,7 +519,7 @@
 
 
 def norm_kernel(parts_ref, owned_ref, squares_ref):
-    owned = jnp.sum(parts_ref[...], axis=0)
+    owned = jnp.sum(parts_ref[...].astype(jnp.float32), axis=0)
     owned_ref[...] = owned
     squares = jnp.sum(jnp.sum(owned * owned, axis=0, keepdims=True), axis=1, keepdims=True)
     squares_ref[...] = jnp.broadcast_to(squares[None], squares_ref.shape)
@@ -573,7 +573,7 @@
     arrived = swap(hold(parts), "fsdp")
     q_grad = turn(turned)
     arrived, q_grad = lax.optimization_barrier((arrived, q_grad))
-    group = jnp.sum(arrived.astype(jnp.float32), axis=0)
+    group = jnp.sum(arrived.astype(jnp.float32), axis=0).astype(jnp.bfloat16)
     owned, squares = norm(swap(jnp.broadcast_to(group, (n_resp,) + group.shape), "resp"), n_fsdp)
     owned, first_term, second_term = lax.optimization_barrier(
         (owned, beta_first * first_moment, beta_second * second_moment)

time: 133 us -> 132 us (level)
  no operation moved by 1% of the time
where the time goes in v5:
time: 132 us
  starting transfers between devices  36.9 us (28%)
  waiting for transfers between devices  35.3 us (27%)
  Pallas kernels  19.4 us (15%)
  between operations  14.8 us (11%)
  blocking collectives  13.9 us (11%)
  local copies, waits for them, and re-layouts  9.8 us (7%)
  other arithmetic  1.5 us (1%)
    all_to_all x3, starting transfers between devices, swap(): return lax.all_to_all(x, axis, 0, 0, tiled=True)  36.9 us
    all_to_all x3, waiting for transfers between devices, swap(): return lax.all_to_all(x, axis, 0, 0, tiled=True)  28.7 us
    all_to_all x1, blocking collectives, swap(): return lax.all_to_all(x, axis, 0, 0, tiled=True)  13.9 us
    unnamed x30, local copies, waits for them, and re-layouts  9.79 us
    pallas_call x1, Pallas kernels, attend(): pl.pallas_call(attend_kernel, out_shape=(jax.ShapeDtypeStruct((n_fsdp, RA...  7.78 us
    all_gather x1, waiting for transfers between devices, on_device(): kv = lax.all_gather(own_kv, 'resp', axis=0, tiled=True)  6.6 us
    pallas_call x1, Pallas kernels, prepare(): pl.pallas_call(prepare_kernel, out_shape=(jax.ShapeDtypeStruct(og.shape,...  3.04 us
  transfers between devices with their start and end apart: 5, of which 4 were waited for; matrix products, arithmetic and copies ran while one was open for 0% of the time, Pallas kernels for 7%

profile of v5, /device:TPU:1, one launch (start us, length us, event | category | flops | bytes accessed | tf_op | source)
XLA Modules:
  0.0 131.7 jit_solution(14480799513070576593)
XLA Ops:
  7.2 1.8 %pack.1 = bf16[144,1024]{1,0:T(8,128)(2,1)} custom-call(bf16[1,128,512]{2,1,0:T(8,128)(2,1)} %rk_ref.1, bf16[1,128,512]{2,1,0:T(8,128)(2,1)} %rv_ref.1, bf16[1,16,512]{2,1,0:T(8,128)(2,1)} %pk_ref.1, bf16[1,16,512]{2,1,0:T(8,128)(2,1)} %pv_ref.1), custom_call_target="tpu_custom_call" | custom-call | flops 1000 | bytes 600000 | tf_op jit(solution)/shard_map/pack/pallas_call | solution.py:464
  9.0 1.4 %shards.1 = bf16[64,16,128]{2,1,0:T(8,128)(2,1)} custom-call(f32[16,120]{1,0:T(8,128)} %adapter_ref.1), custom_call_target="tpu_custom_call" | custom-call | flops 1000 | bytes 300000 | tf_op jit(solution)/shard_map/shards/pallas_call | solution.py:485
  10.5 14.8 %all-to-all-start = ((bf16[64,16,128]{2,1,0:T(8,128)(2,1)}), bf16[64,16,128]{2,1,0:T(8,128)(2,1)S(1)}, u32[]{:S(2)}, u32[]{:S(2)}) async-start(bf16[64,16,128]{2,1,0:T(8,128)(2,1)} %shards.1), calls=%async_computation | async-start | bytes 524288 | tf_op jit(solution)/shard_map/all_to_all | solution.py:551
  26.0 11.3 %all-to-all-done.parts_ref = bf16[64,16,128]{2,1,0:T(8,128)(2,1)S(1)} async-done(((bf16[64,16,128]{2,1,0:T(8,128)(2,1)}), bf16[64,16,128]{2,1,0:T(8,128)(2,1)S(1)}, u32[]{:S(2)}, u32[]{:S(2)}) %all-to-all-start) | async-done | bytes 262176 | tf_op jit(solution)/shard_map/all_to_all | solution.py:551
  37.3 1.1 copy-done.1
  38.4 1.1 copy-done.2
  39.5 0.7 copy-done.3
  40.9 3.0 %prepare.1 = (bf16[128,5120]{1,0:T(8,128)(2,1)S(1)}, bf16[16,128]{1,0:T(8,128)(2,1)S(1)}, bf16[16,2560]{1,0:T(8,128)(2,1)S(1)}, bf16[2560,128]{1,0:T(8,128)(2,1)...) custom-call(s32[1]{0:T(128)} %bitcast.place_ref, ...), custom_call_target="tpu_custom_call" | custom-call | flops 80000000 | bytes 6000000 | tf_op jit(solution)/shard_map/prepare/pallas_call | solution.py:134
  43.9 1.1 copy-done.5
  45.0 0.8 copy-done.6
  45.8 0.8 copy-done.7
  46.7 0.9 copy-done.8
  47.6 0.8 copy-done.9
  50.2 6.6 %all-gather.2.cloned.1.call-done.kv_ref = bf16[1152,1024]{1,0:T(8,128)(2,1)} async-done(((bf16[144,1024]{1,0:T(8,128)(2,1)}), bf16[1152,1024]{1,0:T(8,128)(2,1)}) %all-gather.2.cloned.1.call-update) | async-done | bytes 2359312 | tf_op jit(solution)/shard_map/all_gather | solution.py:563
  56.8 7.8 %attend.1 = (bf16[64,16,128]{2,1,0:T(8,128)(2,1)}, bf16[128,2560]{1,0:T(8,128)(2,1)}, bf16[1152,1024]{1,0:T(8,128)(2,1)}) custom-call(s32[18]{0:T(128)} %copy-done.12, f32[1280,128]{1,0:T(8,128)} %copy-done.9, bf16[2560,128]{1,0:T(8,128)(2,1)} %copy-done.6, bf16[2560,128]{1,0:T(8,128)(2,1)} %copy-done.7, bf16[128,2560]{1,0:T(8,128)(2,1)} %copy-done.8, ...), custom_call_target="tpu_custom_call" | custom-call | flops 3800000000 | bytes 8000000 | tf_op jit(solution)/shard_map/attend/pallas_call | solution.py:370
  64.6 14.2 %all-to-all-start.1 = ((bf16[64,16,128]{2,1,0:T(8,128)(2,1)}), bf16[64,16,128]{2,1,0:T(8,128)(2,1)S(1)}, u32[]{:S(2)}, u32[]{:S(2)}) async-start(bf16[64,16,128]{2,1,0:T(8,128)(2,1)} %hold.1), calls=%async_computation.1 | async-start | bytes 524288 | tf_op jit(solution)/shard_map/all_to_all | solution.py:551
  78.8 2.2 %turn.1 = bf16[128,2560]{1,0:T(8,128)(2,1)} custom-call(bf16[128,2560]{1,0:T(8,128)(2,1)} %get-tuple-element.42.turned_ref), custom_call_target="tpu_custom_call" | custom-call | flops 1000000 | bytes 1300000 | tf_op jit(solution)/shard_map/turn/pallas_call | solution.py:444
  81.0 9.8 %all-to-all-done.1 = bf16[64,16,128]{2,1,0:T(8,128)(2,1)S(1)} async-done(((bf16[64,16,128]{2,1,0:T(8,128)(2,1)}), bf16[64,16,128]{2,1,0:T(8,128)(2,1)S(1)}, u32[]{:S(2)}, u32[]{:S(2)}) %all-to-all-start.1) | async-done | bytes 262176 | tf_op jit(solution)/shard_map/all_to_all | solution.py:551
  90.9 13.9 %all_to_all.20.parts_ref = bf16[8,16,128]{2,1,0:T(8,128)(2,1)} all-to-all(bf16[8,16,128]{2,1,0:T(8,128)(2,1)S(1)} %broadcast_in_dim.7), channel_id=1, replica_groups=mesh['resp'=8,'fsdp'=64] {'resp'}, dimensions={0} | all-to-all | bytes 65536 | tf_op jit(solution)/shard_map/all_to_all | solution.py:551
  104.8 1.5 %norm.1 = (f32[16,128]{1,0:T(8,128)}, f32[64,1,128]{2,1,0:T(1,128)}) custom-call(bf16[8,16,128]{2,1,0:T(8,128)(2,1)} %all_to_all.20.parts_ref), custom_call_target="tpu_custom_call" | custom-call | flops 100000 | bytes 100000 | tf_op jit(solution)/shard_map/norm/pallas_call | solution.py:530
  106.3 7.8 %all-to-all-start.3 = ((f32[64,1,128]{2,1,0:T(1,128)}), f32[64,1,128]{2,1,0:T(1,128)S(1)}, u32[]{:S(2)}, u32[]{:S(2)}) async-start(f32[64,1,128]{2,1,0:T(1,128)} %get-tuple-element.45), calls=%async_computation.3 | async-start | bytes 65536 | tf_op jit(solution)/shard_map/all_to_all | solution.py:551
  114.2 1.7 %unpack.1 = (bf16[1,128,512]{2,1,0:T(8,128)(2,1)}, bf16[1,128,512]{2,1,0:T(8,128)(2,1)}, bf16[1,16,512]{2,1,0:T(8,128)(2,1)}, bf16[1,16,512]{2,1,0:T(8,128)(2,1)}) custom-call(bf16[144,1024]{1,0:T(8,128)(2,1)} %reduce-scatter.2.cloned.1.call-done.kv_ref), custom_call_target="tpu_custom_call" | custom-call | flops 1000 | bytes 600000 | tf_op jit(solution)/shard_map/unpack/pallas_call | solution.py:506
  115.9 7.5 %all-to-all-done.3 = f32[64,1,128]{2,1,0:T(1,128)S(1)} async-done(((f32[64,1,128]{2,1,0:T(1,128)}), f32[64,1,128]{2,1,0:T(1,128)S(1)}, u32[]{:S(2)}, u32[]{:S(2)}) %all-to-all-start.3) | async-done | bytes 32800 | tf_op jit(solution)/shard_map/all_to_all | solution.py:551
  123.5 1.3 %fusion.4 = f32[16,120]{1,0:T(8,128)} fusion(f32[16,120]{1,0:T(8,128)S(1)} %get-tuple-element.59, f32[16,120]{1,0:T(8,128)S(1)} %get-tuple-element.56, f32[16,128]{1,0:T(8,128)} %get-tuple-element.57, f32[120]{0:T(128)S(1)} %divide_bitcast_fusion), kind=kLoop, calls=%fused_computation.5 | loop fusion | flops 19200 | bytes 31200 | tf_op jit(solution)/shard_map/div | solution.py:547
  (33 shorter events, 2.7 us)
Async XLA Ops:
  7.2 30.2 %copy-start = (bf16[1,128,5120]{2,1,0:T(8,128)(2,1)S(1)}, bf16[1,128,5120]{2,1,0:T(8,128)(2,1)}, u32[]{:S(2)}) copy-start(bf16[1,128,5120]{2,1,0:T(8,128)(2,1)} %param.19) | copy-start | bytes 3932164
  7.2 49.6 %all-gather.2.cloned.1.call-start = ((), (), s32[]{:S(2)}) async-start(), calls=%async_computation.5 | async-start | bytes 2654208 | tf_op jit(solution)/shard_map/all_gather | solution.py:563
  10.5 26.8 %all-to-all-start = ((bf16[64,16,128]{2,1,0:T(8,128)(2,1)}), bf16[64,16,128]{2,1,0:T(8,128)(2,1)S(1)}, u32[]{:S(2)}, u32[]{:S(2)}) async-start(bf16[64,16,128]{2,1,0:T(8,128)(2,1)} %shards.1), calls=%async_computation | async-start | bytes 524288 | tf_op jit(solution)/shard_map/all_to_all | solution.py:551
  25.3 88.9 %reduce-scatter.2.cloned.1.call-start = ((), (), s32[]{:S(2)}) async-start(), calls=%async_computation.6 | async-start | bytes 2654208 | tf_op jit(solution)/shard_map/reduce_scatter | solution.py:572
  37.3 1.1 copy-start.1
  38.4 1.1 copy-start.2
  39.5 0.7 copy-start.3
  40.2 0.7 copy-start.4
  43.9 1.1 copy-start.5
  45.0 0.8 copy-start.6
  45.8 0.8 copy-start.7
  46.7 0.9 copy-start.8
  47.6 0.8 copy-start.9
  48.4 0.6 copy-start.10
  49.1 0.6 copy-start.11
  49.7 0.5 copy-start.12
  64.6 49.6 %copy-start.13 = (f32[16,120]{1,0:T(8,128)S(1)}, f32[16,120]{1,0:T(8,128)}, u32[]{:S(2)}) copy-start(f32[16,120]{1,0:T(8,128)} %param.25) | copy-start | bytes 23044
  64.6 49.6 %copy-start.14 = (f32[16,120]{1,0:T(8,128)S(1)}, f32[16,120]{1,0:T(8,128)}, u32[]{:S(2)}) copy-start(f32[16,120]{1,0:T(8,128)} %param.24) | copy-start | bytes 23044
  64.6 26.2 %all-to-all-start.1 = ((bf16[64,16,128]{2,1,0:T(8,128)(2,1)}), bf16[64,16,128]{2,1,0:T(8,128)(2,1)S(1)}, u32[]{:S(2)}, u32[]{:S(2)}) async-start(bf16[64,16,128]{2,1,0:T(8,128)(2,1)} %hold.1), calls=%async_computation.1 | async-start | bytes 524288 | tf_op jit(solution)/shard_map/all_to_all | solution.py:551
  106.3 17.1 %all-to-all-start.3 = ((f32[64,1,128]{2,1,0:T(1,128)}), f32[64,1,128]{2,1,0:T(1,128)S(1)}, u32[]{:S(2)}, u32[]{:S(2)}) async-start(f32[64,1,128]{2,1,0:T(1,128)} %get-tuple-element.45), calls=%async_computation.3 | async-start | bytes 65536 | tf_op jit(solution)/shard_map/all_to_all | solution.py:551
Sparse Core Ops, SparseCore 0:
  10.1 46.6 all-gather.1
  64.7 46.4 reduce-scatter.1
